TPU v7x, 32 devices: a whole 2x2x4 slice. The times are simulated.
32 devices in a mesh: row: 16 (over z, y, x), col: 2 (over core).
Axes of the slice: x: 2, y: 2, z: 4, core: 2. Of those that a mesh axis runs over, the one named last changes fastest.
Arguments:
- tokens: bfloat16 [2048, 1024], P('row', 'col'), may hold values from -6 to 6
- segments: int32 [2048], replicated, may hold values from 0 to 1, as said below
- first_gain: bfloat16 [1024], P('col'), may hold values from 0.5 to 1.5
- in_weight: bfloat16 [1024, 3, 1024], P('row', None, 'col'), may hold values from -0.1875 to 0.1875
- conv_kernel: bfloat16 [3, 1024], P(None, 'col'), may hold values from -4 to 4
- out_weight: bfloat16 [1024, 1024], P('row', 'col'), may hold values from -0.1875 to 0.1875
- second_gain: bfloat16 [1024], P('col'), may hold values from 0.5 to 1.5
- gate_weight: bfloat16 [1024, 4608], P('row', 'col'), may hold values from -0.1875 to 0.1875
- up_weight: bfloat16 [1024, 4608], P('row', 'col'), may hold values from -0.1875 to 0.1875
- down_weight: bfloat16 [4608, 1024], P('row', 'col'), may hold values from -0.09375 to 0.09375
- cotangent: bfloat16 [2048, 1024], P('row', 'col'), may hold values from -6 to 6
Outputs:
- block_out: bfloat16 [2048, 1024], P('row', 'col')
- tokens_grad: float32 [2048, 1024], P('row', 'col')
- first_gain_grad: float32 [1024], P('col')
- in_weight_grad: float32 [1024, 3, 1024], P('row', None, 'col')
- conv_kernel_grad: float32 [3, 1024], P(None, 'col')
- out_weight_grad: float32 [1024, 1024], P('row', 'col')
- second_gain_grad: float32 [1024], P('col')
- gate_weight_grad: float32 [1024, 4608], P('row', 'col')
- up_weight_grad: float32 [1024, 4608], P('row', 'col')
- down_weight_grad: float32 [4608, 1024], P('row', 'col')
Inputs may be any that keep to these rules, and one draw needn't show every extreme that they name: `segments`: segment numbers start at 0, never fall and rise by one at each document start; the largest is reached.
All inputs are finite; a program needn't handle non-finite values.
Results may differ from a plain program's by a relative error of at most 0.0099.
Values may be sent and summed in bfloat16 or wider, within the bound.
A program may use at most 128 MiB of HBM per device.

v0:
```python
import jax
import jax.numpy as jnp
from jax import lax
from jax.sharding import PartitionSpec as P

D = 1024


epsilon = 1e-05


def shifted(block, axis, distance):
    devices = range(lax.axis_size(axis))
    route = [(i - distance, i) for i in devices if i - distance in devices]
    return lax.ppermute(block, axis, route)


def widen(values):
    return lax.all_gather(values, "col", axis=1, tiled=True)


def squares_inverse(values):
    total = lax.psum(jnp.sum(values * values, axis=1), "col")
    return lax.rsqrt(total / D + epsilon)[:, None]


def norm_backward(grad, gain, values, inverse):
    scaled = grad * gain
    total = lax.psum(jnp.sum(scaled * values, axis=1), "col")
    back = inverse * scaled - values * inverse**3 * (total[:, None] / D)
    return (back, jnp.sum(grad * values * inverse, axis=0))


def project(left, weight):
    return jnp.einsum("td,dkc->tkc", left, weight, preferred_element_type=jnp.float32)


def pull(grad, weight):
    partial_sum = jnp.einsum("tkc,dkc->td", grad, weight, preferred_element_type=jnp.float32)
    return lax.psum_scatter(partial_sum, "col", scatter_dimension=1, tiled=True)


def weight_terms(left, grad):
    return lax.psum_scatter(
        jnp.einsum("tr,tkc->rkc", left, grad, preferred_element_type=jnp.float32),
        "row",
        scatter_dimension=0,
        tiled=True,
    )


def local(
    tokens,
    segments,
    first_gain,
    in_weight,
    conv_kernel,
    out_weight,
    second_gain,
    gate_weight,
    up_weight,
    down_weight,
    cotangent,
):
    rows_here = tokens.shape[0]
    tok_float = tokens.astype(jnp.float32)
    gain_one = first_gain.astype(jnp.float32)
    gain_two = second_gain.astype(jnp.float32)
    kernel = conv_kernel.astype(jnp.float32)
    in_full, out_full, gate_full, up_full, down_full = (
        lax.all_gather(in_weight, "row", axis=0, tiled=True),
        lax.all_gather(out_weight, "row", axis=0, tiled=True),
        lax.all_gather(gate_weight, "row", axis=0, tiled=True),
        lax.all_gather(up_weight, "row", axis=0, tiled=True),
        lax.all_gather(down_weight, "row", axis=0, tiled=True),
    )
    pair_weights = jnp.stack([gate_full, up_full], axis=1)
    inv_one = squares_inverse(tok_float)
    normed_one = (tok_float * inv_one * gain_one).astype(jnp.bfloat16)
    normed_one_full = widen(normed_one)
    projected = project(normed_one_full, in_full)
    b_part = projected[:, 0]
    c_part = projected[:, 1]
    x_part = projected[:, 2]
    gated = b_part * x_part
    first_row = lax.axis_index("row") * rows_here
    padded = jnp.concatenate(
        [jnp.full((2,), -1, jnp.int32), segments, jnp.full((2,), -2, jnp.int32)]
    )
    window = lax.dynamic_slice_in_dim(padded, first_row, rows_here + 4)
    own_ids = window[2 : rows_here + 2]
    same_one = (own_ids == window[1 : rows_here + 1]).astype(jnp.float32)[:, None]
    same_two = (own_ids == window[0:rows_here]).astype(jnp.float32)[:, None]
    after_one = (window[3 : rows_here + 3] == own_ids).astype(jnp.float32)[:, None]
    after_two = (window[4 : rows_here + 4] == own_ids).astype(jnp.float32)[:, None]
    earlier = shifted(gated[rows_here - 2 :], "row", 1)
    extended = jnp.concatenate([earlier, gated], axis=0)
    back_one = extended[1 : rows_here + 1] * same_one
    back_two = extended[0:rows_here] * same_two
    mixed = kernel[0] * gated + kernel[1] * back_one + kernel[2] * back_two
    conv_out = (c_part * mixed).astype(jnp.bfloat16)
    conv_full = widen(conv_out)
    attended = project(conv_full, out_full[:, None, :])[:, 0]
    middle = tok_float + attended
    inv_two = squares_inverse(middle)
    normed_two = (middle * inv_two * gain_two).astype(jnp.bfloat16)
    normed_two_full = widen(normed_two)
    both_values = project(normed_two_full, pair_weights)
    gate_value = both_values[:, 0]
    up_value = both_values[:, 1]
    sigma = jax.nn.sigmoid(gate_value)
    activated = gate_value * sigma
    hidden = (activated * up_value).astype(jnp.bfloat16)
    hidden_full = widen(hidden)
    branch_out = project(hidden_full, down_full[:, None, :])[:, 0]
    block_out = (middle + branch_out).astype(jnp.bfloat16)
    cot_three = cotangent[:, None, :]
    hidden_grad = pull(cot_three, down_full[:, None, :])
    down_grad = weight_terms(hidden_full, cot_three)[:, 0]
    gate_grad = hidden_grad * up_value * sigma * (1.0 + gate_value * (1.0 - sigma))
    up_grad = hidden_grad * activated
    pair_grad = jnp.stack([gate_grad, up_grad], axis=1).astype(jnp.bfloat16)
    normed_two_grad = pull(pair_grad, pair_weights)
    pair_weight_grad = weight_terms(normed_two_full, pair_grad)
    middle_back, gain_two_local = norm_backward(normed_two_grad, gain_two, middle, inv_two)
    middle_grad = cotangent.astype(jnp.float32) + middle_back
    attended_grad = middle_grad.astype(jnp.bfloat16)[:, None, :]
    conv_grad = pull(attended_grad, out_full[:, None, :])
    out_grad = weight_terms(conv_full, attended_grad)[:, 0]
    c_grad = conv_grad * mixed
    mixed_grad = conv_grad * c_part
    later = shifted(mixed_grad[0:2], "row", -1)
    ahead = jnp.concatenate([mixed_grad, later], axis=0)
    gated_grad = (
        kernel[0] * mixed_grad
        + kernel[1] * after_one * ahead[1 : rows_here + 1]
        + kernel[2] * after_two * ahead[2 : rows_here + 2]
    )
    kernel_local = jnp.stack(
        [
            jnp.sum(mixed_grad * gated, axis=0),
            jnp.sum(mixed_grad * back_one, axis=0),
            jnp.sum(mixed_grad * back_two, axis=0),
        ]
    )
    projected_grad = jnp.stack([gated_grad * x_part, c_grad, gated_grad * b_part], axis=1).astype(
        jnp.bfloat16
    )
    normed_one_grad = pull(projected_grad, in_full)
    in_grad = weight_terms(normed_one_full, projected_grad)
    token_back, gain_one_local = norm_backward(normed_one_grad, gain_one, tok_float, inv_one)
    tokens_grad = middle_grad + token_back
    gain_one_grad, kernel_grad, gain_two_grad = lax.psum(
        (gain_one_local, kernel_local, gain_two_local), "row"
    )
    return (
        block_out,
        tokens_grad,
        gain_one_grad,
        in_grad,
        kernel_grad,
        out_grad,
        gain_two_grad,
        pair_weight_grad[:, 0],
        pair_weight_grad[:, 1],
        down_grad,
    )


def solution(mesh):
    in_specs = (
        P("row", "col"),
        P(),
        P("col"),
        P("row", None, "col"),
        P(None, "col"),
        P("row", "col"),
        P("col"),
        P("row", "col"),
        P("row", "col"),
        P("row", "col"),
        P("row", "col"),
    )
    out_specs = (
        P("row", "col"),
        P("row", "col"),
        P("col"),
        P("row", None, "col"),
        P(None, "col"),
        P("row", "col"),
        P("col"),
        P("row", "col"),
        P("row", "col"),
        P("row", "col"),
    )
    return jax.shard_map(local, mesh=mesh, in_specs=in_specs, out_specs=out_specs, check_vma=False)
```

profile of v0, /device:TPU:0, one launch (start us, length us, event | category | flops | bytes accessed | tf_op | source)
XLA Modules:
  0.0 1152.6 jit_solution(18219568011532345377)
XLA Ops:
  10.6 83.4 %all-gather.17.cloned.1.call-done = bf16[4608,512]{1,0:T(8,128)(2,1)} async-done(((bf16[288,512]{1,0:T(8,128)(2,1)}), bf16[4608,512]{1,0:T(8,128)(2,1)}) %all-gather.17.cloned.1.call-update) | async-done | bytes 4718608 | tf_op jit(solution)/shard_map/all_gather | solution.py:75
  94.0 5.4 fusion.47
  100.5 2.5 psum.49
  103.7 2.0 all_gather.27
  105.7 57.3 %all-gather.7.cloned.1.call-done = bf16[1024,3,512]{2,0,1:T(8,128)(2,1)} async-done(((bf16[64,3,512]{2,0,1:T(8,128)(2,1)}), bf16[1024,3,512]{2,0,1:T(8,128)(2,1)}) %all-gather.7.cloned.1.call-update) | async-done | bytes 3145744 | tf_op jit(solution)/shard_map/all_gather | solution.py:71
  163.0 2.5 fusion.29
  165.6 3.4 collective-permute-start
  173.1 47.1 %all-gather.9.cloned.1.call-done = bf16[1024,512]{1,0:T(8,128)(2,1)} async-done(((bf16[64,512]{1,0:T(8,128)(2,1)}), bf16[1024,512]{1,0:T(8,128)(2,1)}) %all-gather.9.cloned.1.call-update) | async-done | bytes 1048592 | tf_op jit(solution)/shard_map/all_gather | solution.py:72
  221.8 2.5 psum.50
  224.4 2.0 all_gather.31
  226.4 75.8 %all-gather.11.cloned.1.call-done = bf16[1024,2304]{1,0:T(8,128)(2,1)} async-done(((bf16[64,2304]{1,0:T(8,128)(2,1)}), bf16[1024,2304]{1,0:T(8,128)(2,1)}) %all-gather.11.cloned.1.call-update) | async-done | bytes 4718608 | tf_op jit(solution)/shard_map/all_gather | solution.py:73
  302.1 81.8 %all-gather.13.cloned.1.call-done = bf16[1024,2304]{1,0:T(8,128)(2,1)} async-done(((bf16[64,2304]{1,0:T(8,128)(2,1)}), bf16[1024,2304]{1,0:T(8,128)(2,1)}) %all-gather.13.cloned.1.call-update) | async-done | bytes 4718608 | tf_op jit(solution)/shard_map/all_gather | solution.py:74
  383.9 4.6 fusion.1
  388.5 6.0 reduce-scatter.9.cloned.1.call-done
  394.6 2.9 fusion.7
  398.5 6.4 fusion.2
  405.0 9.2 reduce-scatter.11.cloned.1.call-done
  415.8 2.4 psum.51
  422.2 8.5 reduce-scatter.13.cloned.1.call-done
  430.6 2.1 multiply_reduce_fusion.2
  434.1 4.2 collective-permute-done.1
  443.2 10.4 fusion.5
  456.7 3.6 fusion.27
  461.2 6.3 convolution_bitcast_fusion
  468.9 4.3 fusion.4
  474.3 2.5 psum.52
  476.8 79.7 %all-reduce = (f32[512]{0:T(512)}, f32[3,512]{1,0:T(4,128)}, f32[512]{0:T(512)}) all-reduce(f32[512]{0:T(512)S(1)} %get-tuple-element.15, f32[3,512]{1,0:T(4,128)S(1)} %pad_maximum_fusion.13, f32[512]{0:T(512)S(1)} %copy-done.28), channel_id=1, replica_groups=mesh['row'=16,'col'=2] {'row'}, use_global_device_ids=true, to_apply=%region_13.0 | all-reduce | flops 2560 | bytes 20480 | tf_op jit(solution)/shard_map/psum | solution.py:153
  558.2 190.6 %reduce-scatter.21.cloned.1.call-done = f32[64,2,2304]{2,0,1:T(8,128)} async-done(((f32[1024,2,2304]{2,0,1:T(8,128)}), f32[64,2,2304]{2,0,1:T(8,128)}) %reduce-scatter.21.cloned.1.call-update) | async-done | bytes 1179664 | tf_op jit(solution)/shard_map/reduce_scatter | solution.py:44
  748.8 2.3 slice_bitcast_fusion.2
  751.1 80.1 %reduce-scatter.19.cloned.1.call-done = f32[64,1,512]{2,0,1:T(8,128)} async-done(((f32[1024,1,512]{2,0,1:T(8,128)}), f32[64,1,512]{2,0,1:T(8,128)}) %reduce-scatter.19.cloned.1.call-update) | async-done | bytes 131088 | tf_op jit(solution)/shard_map/reduce_scatter | solution.py:44
  831.2 136.5 %reduce-scatter.17.cloned.1.call-done = f32[64,3,512]{2,0,1:T(8,128)} async-done(((f32[1024,3,512]{2,0,1:T(8,128)}), f32[64,3,512]{2,0,1:T(8,128)}) %reduce-scatter.17.cloned.1.call-update) | async-done | bytes 393232 | tf_op jit(solution)/shard_map/reduce_scatter | solution.py:44
  967.7 178.3 %reduce-scatter.23.cloned.1.call-done = f32[288,1,512]{2,0,1:T(8,128)} async-done(((f32[4608,1,512]{2,0,1:T(8,128)}), f32[288,1,512]{2,0,1:T(8,128)}) %reduce-scatter.23.cloned.1.call-update) | async-done | bytes 589840 | tf_op jit(solution)/shard_map/reduce_scatter | solution.py:44
  (139 shorter events, 31.8 us)
Async XLA Ops:
  7.2 86.8 %all-gather.17.cloned.1.call-start = ((), (), s32[]{:S(2)}) async-start(), calls=%async_computation.13 | async-start | bytes 5013504 | tf_op jit(solution)/shard_map/all_gather | solution.py:75
  7.9 155.1 %all-gather.7.cloned.1.call-start = ((), (), s32[]{:S(2)}) async-start(), calls=%async_computation.8 | async-start | bytes 3342336 | tf_op jit(solution)/shard_map/all_gather | solution.py:71
  8.7 211.5 %all-gather.9.cloned.1.call-start = ((), (), s32[]{:S(2)}) async-start(), calls=%async_computation.9 | async-start | bytes 1114112 | tf_op jit(solution)/shard_map/all_gather | solution.py:72
  9.4 292.7 %all-gather.11.cloned.1.call-start = ((), (), s32[]{:S(2)}) async-start(), calls=%async_computation.10 | async-start | bytes 5013504 | tf_op jit(solution)/shard_map/all_gather | solution.py:73
  10.0 373.9 %all-gather.13.cloned.1.call-start = ((), (), s32[]{:S(2)}) async-start(), calls=%async_computation.11 | async-start | bytes 5013504 | tf_op jit(solution)/shard_map/all_gather | solution.py:74
  10.6 384.0 %reduce-scatter.9.cloned.1.call-start = ((), (), s32[]{:S(2)}) async-start(), calls=%async_computation.14 | async-start | bytes 3538944 | tf_op jit(solution)/shard_map/reduce_scatter | solution.py:40
  99.5 6.2 copy-start.24
  99.5 314.7 %reduce-scatter.11.cloned.1.call-start = ((), (), s32[]{:S(2)}) async-start(), calls=%async_computation.15 | async-start | bytes 786432 | tf_op jit(solution)/shard_map/reduce_scatter | solution.py:40
  103.6 61.9 %copy-start.32 = (f32[128]{0:T(128)}, f32[128]{0:T(128)S(1)}, u32[]{:S(2)}) copy-start(f32[128]{0:T(128)S(1)} %get-tuple-element.39) | copy-start | bytes 1540
  105.7 59.9 %copy-start.8 = (bf16[128,1024]{1,0:T(8,128)(2,1)}, bf16[128,1024]{1,0:T(8,128)(2,1)S(1)}, u32[]{:S(2)}) copy-start(bf16[128,1024]{1,0:T(8,128)(2,1)S(1)} %all_gather.27) | copy-start | bytes 786436
  105.7 63.9 %copy-start.35 = (bf16[512]{0:T(512)(128)(2,1)S(1)}, bf16[512]{0:T(512)(128)(2,1)}, u32[]{:S(2)}) copy-start(bf16[512]{0:T(512)(128)(2,1)} %param.17) | copy-start | bytes 3076
  165.6 5.6 copy-start.7
  165.6 4.7 collective-permute-start
  169.5 218.9 %copy-start.30 = (f32[128]{0:T(128)}, f32[128]{0:T(128)S(1)}, u32[]{:S(2)}) copy-start(f32[128]{0:T(128)S(1)} %get-tuple-element.35) | copy-start | bytes 1540
  169.6 218.9 %copy-start.31 = (f32[128]{0:T(128)}, f32[128]{0:T(128)S(1)}, u32[]{:S(2)}) copy-start(f32[128]{0:T(128)S(1)} %get-tuple-element.36) | copy-start | bytes 1540
  170.3 218.2 %copy-start.23 = (f32[2,512]{1,0:T(2,128)}, f32[2,512]{1,0:T(2,128)S(1)}, u32[]{:S(2)}) copy-start(f32[2,512]{1,0:T(2,128)S(1)} %collective-permute-done) | copy-start | bytes 12292
  173.1 215.4 %copy-start.10 = (bf16[128,1024]{1,0:T(8,128)(2,1)}, bf16[128,1024]{1,0:T(8,128)(2,1)S(1)}, u32[]{:S(2)}) copy-start(bf16[128,1024]{1,0:T(8,128)(2,1)S(1)} %all_gather.29) | copy-start | bytes 786436
  226.4 162.1 %copy-start.14 = (bf16[128,1024]{1,0:T(8,128)(2,1)}, bf16[128,1024]{1,0:T(8,128)(2,1)S(1)}, u32[]{:S(2)}) copy-start(bf16[128,1024]{1,0:T(8,128)(2,1)S(1)} %all_gather.31) | copy-start | bytes 786436
  398.5 19.8 %copy-start.15 = (bf16[128,512]{1,0:T(8,128)(2,1)S(1)}, bf16[128,512]{1,0:T(8,128)(2,1)}, u32[]{:S(2)}) copy-start(bf16[128,512]{1,0:T(8,128)(2,1)} %param.21) | copy-start | bytes 393220
  404.9 15.2 %copy-start.3 = (bf16[1024,512]{1,0:T(8,128)(2,1)S(1)}, bf16[1024,512]{1,0:T(8,128)(2,1)}, u32[]{:S(2)}) copy-start(bf16[1024,512]{1,0:T(8,128)(2,1)} %all-gather.9.cloned.1.call-done) | copy-start | bytes 3145732
  404.9 25.7 %reduce-scatter.13.cloned.1.call-start = ((), (), s32[]{:S(2)}) async-start(), calls=%async_computation.16 | async-start | bytes 786432 | tf_op jit(solution)/shard_map/reduce_scatter | solution.py:40
  421.4 19.8 %copy-start = (bf16[1024,3,512]{2,0,1:T(8,128)(2,1)S(1)}, bf16[1024,3,512]{2,0,1:T(8,128)(2,1)}, u32[]{:S(2)}) copy-start(bf16[1024,3,512]{2,0,1:T(8,128)(2,1)} %all-gather.7.cloned.1.call-done) | copy-start | bytes 9437188
  421.4 39.0 %all-gather.15.cloned.1.call-start = ((), (), s32[]{:S(2)}) async-start(), calls=%async_computation.12 | async-start | bytes 1769472 | tf_op jit(solution)/shard_map/all_gather | solution.py:19
  422.1 51.1 %reduce-scatter.15.cloned.1.call-start = ((), (), s32[]{:S(2)}) async-start(), calls=%async_computation.17 | async-start | bytes 786432 | tf_op jit(solution)/shard_map/reduce_scatter | solution.py:40
  432.8 7.7 copy-start.17
  432.8 5.5 collective-permute-start.1
  443.1 305.7 %reduce-scatter.21.cloned.1.call-start = ((), (), s32[]{:S(2)}) async-start(), calls=%async_computation.20 | async-start | bytes 20054016 | tf_op jit(solution)/shard_map/reduce_scatter | solution.py:44
  453.7 377.6 %reduce-scatter.19.cloned.1.call-start = ((), (), s32[]{:S(2)}) async-start(), calls=%async_computation.19 | async-start | bytes 2228224 | tf_op jit(solution)/shard_map/reduce_scatter | solution.py:44
  456.4 511.3 %reduce-scatter.17.cloned.1.call-start = ((), (), s32[]{:S(2)}) async-start(), calls=%async_computation.18 | async-start | bytes 6684672 | tf_op jit(solution)/shard_map/reduce_scatter | solution.py:44
  460.3 685.7 %reduce-scatter.23.cloned.1.call-start = ((), (), s32[]{:S(2)}) async-start(), calls=%async_computation.21 | async-start | bytes 10027008 | tf_op jit(solution)/shard_map/reduce_scatter | solution.py:44
  468.8 7.9 copy-start.28
  468.9 87.6 %copy-start.36 = (f32[128]{0:T(128)S(1)}, f32[128]{0:T(128)}, u32[]{:S(2)}) copy-start(f32[128]{0:T(128)} %get-tuple-element.38) | copy-start | bytes 1540
  (22 other events, 48.7 us)
Sparse Core Ops, SparseCore 0:
  10.8 83.1 all-gather.16
  96.8 66.2 all-gather.6
  165.8 54.3 all-gather.8
  222.8 79.2 all-gather.10
  304.8 79.0 all-gather.12
  386.0 8.5 reduce-scatter.8
  405.0 9.1 reduce-scatter.10
  421.5 9.0 reduce-scatter.12
  432.8 10.3 all-gather.14
  445.4 9.1 reduce-scatter.14
  460.3 288.4 reduce-scatter.20
  751.5 79.6 reduce-scatter.18
  834.1 133.5 reduce-scatter.16
  973.8 172.1 reduce-scatter.22
where the time goes:
time: 1150 us
  waiting for transfers between devices  963 us (84%)
  blocking collectives  95.5 us (8%)
  matrix products  50.1 us (4%)
  other arithmetic  15.3 us (1%)
  between operations  14.3 us (1%)
    reduce_scatter x4, waiting for transfers between devices, weight_terms(): lax.psum_scatter(jnp.einsum('tr,tkc->rkc', left, grad, preferred_element_...  585 us
    all_gather x1, waiting for transfers between devices, local(): lax.all_gather(down_weight, 'row', axis=0, tiled=True)  83.4 us
    all_gather x1, waiting for transfers between devices, local(): lax.all_gather(up_weight, 'row', axis=0, tiled=True)  81.8 us
    psum x1, blocking collectives, local(): lax.psum((gain_one_local, kernel_local, gain_two_local), 'row')  79.7 us
    all_gather x1, waiting for transfers between devices, local(): lax.all_gather(gate_weight, 'row', axis=0, tiled=True)  75.8 us
    all_gather x1, waiting for transfers between devices, local(): lax.all_gather(in_weight, 'row', axis=0, tiled=True)  57.3 us
    all_gather x1, waiting for transfers between devices, local(): lax.all_gather(out_weight, 'row', axis=0, tiled=True)  47.1 us
    reduce_scatter x4, waiting for transfers between devices, pull(): return lax.psum_scatter(partial_sum, 'col', scatter_dimension=1, tiled=True)  23.8 us
  transfers between devices with their start and end apart: 16, of which 14 were waited for; matrix products, arithmetic and copies ran while one was open for 5% of the time, Pallas kernels for 0%

commit v1 on v0

--- a/solution.py
+++ b/solution.py
@@ -1,6 +1,10 @@
+import functools
+
 import jax
 import jax.numpy as jnp
 from jax import lax
+from jax.experimental import pallas as pl
+from jax.experimental.pallas import tpu as pltpu
 from jax.sharding import PartitionSpec as P
 
 D = 1024
@@ -167,6 +171,441 @@
     )
 
 
+MESH = pl.DeviceIdType.MESH
+VMEM = pl.BlockSpec(memory_space=pltpu.VMEM)
+ANY = pl.BlockSpec(memory_space=pl.ANY)
+
+
+def greet(devices):
+    barrier = pltpu.get_barrier_semaphore()
+    for device in devices:
+        pl.semaphore_signal(barrier, inc=1, device_id=device, device_id_type=MESH)
+    pl.semaphore_wait(barrier, len(devices))
+
+
+def remote(source, target, send, receive, device):
+    return pltpu.make_async_remote_copy(
+        src_ref=source,
+        dst_ref=target,
+        send_sem=send,
+        recv_sem=receive,
+        device_id=device,
+        device_id_type=MESH,
+    )
+
+
+def gather_kernel(team, cols, count, *refs):
+    ins, outs = refs[:count], refs[count : 2 * count]
+    send, recv, pass_send, pass_recv, own_sem = refs[2 * count :]
+    row, col = lax.axis_index("row"), lax.axis_index("col")
+    place = lax.rem(row, team)
+    first = row - place
+    mates = [first + lax.rem(place + k, team) for k in range(1, team)]
+    others = [lax.rem(col + j, cols) for j in range(1, cols)]
+    greet([(mate, col) for mate in mates] + [(row, other) for other in others])
+
+    def slot(i, which, side):
+        tall, wide = ins[i].shape
+        return outs[i].at[
+            pl.ds(pl.multiple_of(which * tall, tall), tall),
+            pl.ds(pl.multiple_of(side * wide, wide), wide),
+        ]
+
+    sends, passes, locals_ = {}, {}, []
+    for i in range(count):
+        for k in range(1, team):
+            sends[i, k] = remote(
+                ins[i], slot(i, place, col), send.at[i, k], recv.at[i, k], (mates[k - 1], col)
+            )
+            sends[i, k].start()
+        for j in range(1, cols):
+            passes[i, 0, j] = remote(
+                ins[i],
+                slot(i, place, col),
+                pass_send.at[i, 0, j],
+                pass_recv.at[i, 0, j],
+                (row, others[j - 1]),
+            )
+            passes[i, 0, j].start()
+        copy = pltpu.make_async_copy(ins[i], slot(i, place, col), own_sem.at[i])
+        copy.start()
+        locals_.append(copy)
+    for i in range(count):
+        for k in range(1, team):
+            origin = lax.rem(place - k + team, team)
+            arrived = slot(i, origin, col)
+            remote(arrived, arrived, send.at[i, k], recv.at[i, k], (mates[k - 1], col)).wait_recv()
+            for j in range(1, cols):
+                passes[i, k, j] = remote(
+                    arrived,
+                    arrived,
+                    pass_send.at[i, k, j],
+                    pass_recv.at[i, k, j],
+                    (row, others[j - 1]),
+                )
+                passes[i, k, j].start()
+    for (i, k, j), copy in passes.items():
+        origin = lax.rem(place - k + team, team)
+        landed = slot(i, origin, lax.rem(col - j + cols, cols))
+        remote(
+            landed, landed, pass_send.at[i, k, j], pass_recv.at[i, k, j], (row, others[j - 1])
+        ).wait_recv()
+    for copy in passes.values():
+        copy.wait_send()
+    for copy in sends.values():
+        copy.wait_send()
+    for copy in locals_:
+        copy.wait()
+
+
+def gather(blocks, team, cols, identity):
+    count = len(blocks)
+    return pl.pallas_call(
+        functools.partial(gather_kernel, team, cols, count),
+        out_shape=[
+            jax.ShapeDtypeStruct((b.shape[0] * team, b.shape[1] * cols), b.dtype) for b in blocks
+        ],
+        in_specs=[ANY] * count,
+        out_specs=[ANY] * count,
+        scratch_shapes=[
+            pltpu.SemaphoreType.DMA((count, team)),
+            pltpu.SemaphoreType.DMA((count, team)),
+            pltpu.SemaphoreType.DMA((count, team, cols)),
+            pltpu.SemaphoreType.DMA((count, team, cols)),
+            pltpu.SemaphoreType.DMA((count,)),
+        ],
+        compiler_params=pltpu.CompilerParams(collective_id=identity, has_side_effects=True),
+    )(*blocks)
+
+
+def scatter_kernel(
+    team, cols, x_ref, o_ref, inbox, stage, land, send, recv, pass_send, pass_recv
+):
+    row, col = lax.axis_index("row"), lax.axis_index("col")
+    place = lax.rem(row, team)
+    first = row - place
+    mates = [first + lax.rem(place + k, team) for k in range(1, team)]
+    others = [lax.rem(col + j, cols) for j in range(1, cols)]
+    greet([(mate, col) for mate in mates] + [(row, other) for other in others])
+    tall, wide = o_ref.shape
+
+    def part(k, side):
+        return x_ref.at[
+            pl.ds(pl.multiple_of(lax.rem(place + k, team) * tall, tall), tall),
+            pl.ds(pl.multiple_of(side * wide, wide), wide),
+        ]
+
+    order = list(range(1, team)) + [0]
+    passes, sends = {}, {}
+    for k in order:
+        for j in range(1, cols):
+            passes[k, j] = remote(
+                part(k, others[j - 1]),
+                inbox.at[j - 1, k],
+                pass_send.at[k, j],
+                pass_recv.at[k, j],
+                (row, others[j - 1]),
+            )
+            passes[k, j].start()
+    for k in order:
+        total = part(k, col)[...].astype(jnp.float32)
+        for j in range(1, cols):
+            passes[k, j].wait_recv()
+            total = total + inbox[j - 1, k].astype(jnp.float32)
+        if k:
+            stage[k - 1] = total.astype(jnp.bfloat16)
+            sends[k] = remote(
+                stage.at[k - 1], land.at[k - 1], send.at[k], recv.at[k], (mates[k - 1], col)
+            )
+            sends[k].start()
+        else:
+            o_ref[...] = total
+    for k in range(1, team):
+        sends[k].wait_recv()
+        o_ref[...] += land[k - 1].astype(jnp.float32)
+    for copy in passes.values():
+        copy.wait_send()
+    for copy in sends.values():
+        copy.wait_send()
+
+
+def scatter(partial_sum, team, cols, identity):
+    tall, wide = partial_sum.shape[0] // team, partial_sum.shape[1] // cols
+    return pl.pallas_call(
+        functools.partial(scatter_kernel, team, cols),
+        out_shape=jax.ShapeDtypeStruct((tall, wide), jnp.float32),
+        in_specs=[VMEM],
+        out_specs=VMEM,
+        scratch_shapes=[
+            pltpu.VMEM((cols - 1, team, tall, wide), jnp.bfloat16),
+            pltpu.VMEM((team - 1, tall, wide), jnp.bfloat16),
+            pltpu.VMEM((team - 1, tall, wide), jnp.bfloat16),
+            pltpu.SemaphoreType.DMA((team,)),
+            pltpu.SemaphoreType.DMA((team,)),
+            pltpu.SemaphoreType.DMA((team, cols)),
+            pltpu.SemaphoreType.DMA((team, cols)),
+        ],
+        compiler_params=pltpu.CompilerParams(
+            collective_id=identity, has_side_effects=True, vmem_limit_bytes=24 * 2**20
+        ),
+    )(partial_sum)
+
+
+def exchange_kernel(
+    team, cols, outward, wide_ref, tall_ref, wide_out, tall_out, send, recv, t_send, t_recv, own
+):
+    rows = team * cols
+    row, col = lax.axis_index("row"), lax.axis_index("col")
+    place = lax.rem(row, team)
+    group = lax.div(row, team)
+    peers = [lax.rem(row + k, rows) for k in range(1, rows)]
+    greet(
+        [(peer, col) for peer in peers]
+        + [
+            (lax.rem(group + m, cols) * team + place, lax.rem(col + j, cols))
+            for m in range(cols)
+            for j in range(1, cols)
+        ]
+    )
+    home = group == col
+
+    def target(m):
+        if outward:
+            return lax.rem(group + m, cols) * team + place, group
+        return col * team + place, lax.rem(col + m, cols)
+
+    def tall_copy(m):
+        if outward:
+            source, landing, index = tall_ref, tall_out.at[col], col
+        else:
+            source, landing, index = tall_ref.at[lax.rem(col + m, cols)], tall_out.at[group], group
+        return remote(source, landing, t_send.at[m], t_recv.at[index], target(m))
+
+    def tall_own():
+        source = tall_ref if outward else tall_ref.at[col]
+        return pltpu.make_async_copy(source, tall_out.at[col], own.at[1])
+
+    def wide_source(peer):
+        return wide_ref.at[lax.rem(peer, team) if outward else peer]
+
+    copies = []
+    for k in range(1, rows):
+        peer = peers[k - 1]
+        copy = remote(
+            wide_source(peer), wide_out.at[row], send.at[k], recv.at[k], (peer, col)
+        )
+        copy.start()
+        copies.append(copy)
+    mine = pltpu.make_async_copy(wide_source(row), wide_out.at[row], own.at[0])
+    mine.start()
+    for m in range(cols):
+        if m:
+            tall_copy(m).start()
+        else:
+            pl.when(home)(lambda: tall_own().start())
+            pl.when(jnp.logical_not(home))(lambda: tall_copy(0).start())
+    for k in range(1, rows):
+        landed = wide_out.at[lax.rem(row - k + rows, rows)]
+        remote(landed, landed, send.at[k], recv.at[k], (peers[k - 1], col)).wait_recv()
+    for j in range(cols):
+        landed = tall_out.at[j]
+        arriving = remote(landed, landed, t_send.at[0], t_recv.at[j], target(1))
+        is_own = jnp.logical_and(home, col == j)
+        pl.when(is_own)(lambda: tall_own().wait())
+        pl.when(jnp.logical_not(is_own))(lambda arriving=arriving: arriving.wait_recv())
+    for copy in copies:
+        copy.wait_send()
+    mine.wait()
+    for m in range(cols):
+        if m:
+            tall_copy(m).wait_send()
+        else:
+            pl.when(jnp.logical_not(home))(lambda: tall_copy(0).wait_send())
+
+
+def exchange(wide, tall, team, cols, outward, identity):
+    rows = team * cols
+    return pl.pallas_call(
+        functools.partial(exchange_kernel, team, cols, outward),
+        out_shape=[
+            jax.ShapeDtypeStruct((rows,) + wide.shape[1:], wide.dtype),
+            jax.ShapeDtypeStruct((cols,) + tall.shape[-2:], tall.dtype),
+        ],
+        in_specs=[ANY] * 2,
+        out_specs=[ANY] * 2,
+        scratch_shapes=[
+            pltpu.SemaphoreType.DMA((rows,)),
+            pltpu.SemaphoreType.DMA((rows,)),
+            pltpu.SemaphoreType.DMA((cols,)),
+            pltpu.SemaphoreType.DMA((cols,)),
+            pltpu.SemaphoreType.DMA((2,)),
+        ],
+        compiler_params=pltpu.CompilerParams(collective_id=identity, has_side_effects=True),
+    )(wide, tall)
+
+
+def dot(a, b, a_dim, b_dim, kind=jnp.float32):
+    out = lax.dot_general(
+        a, b, (((a_dim,), (b_dim,)), ((), ())), preferred_element_type=jnp.float32
+    )
+    return out.astype(kind)
+
+
+def teams(
+    tokens,
+    segments,
+    first_gain,
+    in_weight,
+    conv_kernel,
+    out_weight,
+    second_gain,
+    gate_weight,
+    up_weight,
+    down_weight,
+    cotangent,
+):
+    bf = jnp.bfloat16
+    rows, cols = lax.axis_size("row"), lax.axis_size("col")
+    team = rows // cols
+    row, col = lax.axis_index("row"), lax.axis_index("col")
+    place, group = lax.rem(row, team), lax.div(row, team)
+    depth, _, width = in_weight.shape
+    inner = gate_weight.shape[1]
+    thin, part = width // team, inner // team
+    held = tokens.shape[0] * team
+    blocks = in_weight.reshape(depth, 3, team, thin).transpose(2, 0, 1, 3)
+    wide = jnp.concatenate(
+        [
+            blocks.reshape(team, depth, 3 * thin),
+            gate_weight.reshape(depth, team, part).transpose(1, 0, 2),
+            up_weight.reshape(depth, team, part).transpose(1, 0, 2),
+        ],
+        axis=2,
+    )
+    tall = jnp.concatenate([out_weight, down_weight], axis=0)
+    tok_float = tokens.astype(jnp.float32)
+    gain_one = first_gain.astype(jnp.float32)
+    gain_two = second_gain.astype(jnp.float32)
+    kernel = lax.dynamic_slice_in_dim(conv_kernel, place * thin, thin, 1).astype(jnp.float32)
+    inv_one = squares_inverse(tok_float)
+    normed_one = (tok_float * inv_one * gain_one).astype(bf)
+
+    wide_all, tall_all = exchange(wide, tall, team, cols, True, 1)
+    wide_all = wide_all.reshape(rows * depth, 3 * thin + 2 * part)
+    in_part, pair_part = wide_all[:, : 3 * thin], wide_all[:, 3 * thin :]
+    tall_all = tall_all.transpose(1, 0, 2).reshape(tall.shape[0], cols * width)
+    out_part, down_part = tall_all[:depth], tall_all[depth:]
+    normed_full, cot_full = gather([normed_one, cotangent], team, cols, 2)
+
+    projected = dot(normed_full, in_part, 1, 0)
+    b_part = projected[:, :thin]
+    c_part = projected[:, thin : 2 * thin]
+    x_part = projected[:, 2 * thin :]
+    gated = b_part * x_part
+    padded = jnp.concatenate(
+        [jnp.full((2,), -1, jnp.int32), segments, jnp.full((2,), -2, jnp.int32)]
+    )
+    window = lax.dynamic_slice_in_dim(padded, group * held, held + 4)
+    own_ids = window[2 : held + 2]
+    same_one = (own_ids == window[1 : held + 1]).astype(jnp.float32)[:, None]
+    same_two = (own_ids == window[0:held]).astype(jnp.float32)[:, None]
+    after_one = (window[3 : held + 3] == own_ids).astype(jnp.float32)[:, None]
+    after_two = (window[4 : held + 4] == own_ids).astype(jnp.float32)[:, None]
+    earlier = shifted(gated[held - 2 :], "row", team)
+    extended = jnp.concatenate([earlier, gated], axis=0)
+    back_one = extended[1 : held + 1] * same_one
+    back_two = extended[0:held] * same_two
+    mixed = kernel[0] * gated + kernel[1] * back_one + kernel[2] * back_two
+    conv_out = (c_part * mixed).astype(bf)
+    attended = scatter(dot(conv_out, out_part, 1, 0, bf), team, cols, 3)
+    middle = tok_float + attended
+    inv_two = squares_inverse(middle)
+    normed_two = (middle * inv_two * gain_two).astype(bf)
+    (two_full,) = gather([normed_two], team, cols, 4)
+    both = dot(two_full, pair_part, 1, 0)
+    gate_value, up_value = both[:, :part], both[:, part:]
+    sigma = jax.nn.sigmoid(gate_value)
+    activated = gate_value * sigma
+    hidden = (activated * up_value).astype(bf)
+    hidden_grad = dot(cot_full, down_part, 1, 1)
+    gate_grad = hidden_grad * up_value * sigma * (1.0 + gate_value * (1.0 - sigma))
+    up_grad = hidden_grad * activated
+    pair_grad = jnp.concatenate([gate_grad.astype(bf), up_grad.astype(bf)], axis=1)
+    normed_two_grad = scatter(dot(pair_grad, pair_part, 1, 1, bf), team, cols, 5)
+    branch_out = scatter(dot(hidden, down_part, 1, 0, bf), team, cols, 6)
+    block_out = (middle + branch_out).astype(bf)
+    middle_back, gain_two_local = norm_backward(normed_two_grad, gain_two, middle, inv_two)
+    middle_grad = cotangent.astype(jnp.float32) + middle_back
+    (attended_grad,) = gather([middle_grad.astype(bf)], team, cols, 7)
+    conv_grad = dot(attended_grad, out_part, 1, 1)
+    c_grad = conv_grad * mixed
+    mixed_grad = conv_grad * c_part
+    later = shifted(mixed_grad[0:2], "row", -team)
+    ahead = jnp.concatenate([mixed_grad, later], axis=0)
+    gated_grad = (
+        kernel[0] * mixed_grad
+        + kernel[1] * after_one * ahead[1 : held + 1]
+        + kernel[2] * after_two * ahead[2 : held + 2]
+    )
+    kernel_local = jnp.stack(
+        [
+            jnp.sum(mixed_grad * gated, axis=0),
+            jnp.sum(mixed_grad * back_one, axis=0),
+            jnp.sum(mixed_grad * back_two, axis=0),
+        ]
+    )
+    kernel_local = lax.dynamic_update_slice_in_dim(
+        jnp.zeros((3, width), jnp.float32), kernel_local, place * thin, 1
+    )
+    projected_grad = jnp.concatenate(
+        [
+            (gated_grad * x_part).astype(bf),
+            c_grad.astype(bf),
+            (gated_grad * b_part).astype(bf),
+        ],
+        axis=1,
+    )
+    normed_one_grad = scatter(dot(projected_grad, in_part, 1, 1, bf), team, cols, 8)
+    token_back, gain_one_local = norm_backward(normed_one_grad, gain_one, tok_float, inv_one)
+    tokens_grad = middle_grad + token_back
+
+    wide_grad = jnp.concatenate(
+        [dot(normed_full, projected_grad, 0, 0, bf), dot(two_full, pair_grad, 0, 0, bf)], axis=1
+    ).reshape(rows, depth, 3 * thin + 2 * part)
+    tall_grad = jnp.concatenate(
+        [dot(conv_out, attended_grad, 0, 0, bf), dot(hidden, cot_full, 0, 0, bf)], axis=0
+    )
+    tall_grad = tall_grad.reshape(tall.shape[0], cols, width).transpose(1, 0, 2)
+    wide_back, tall_back = exchange(wide_grad, tall_grad, team, cols, False, 9)
+    wide_sum = jnp.sum(
+        wide_back.astype(jnp.float32).reshape(cols, team, depth, 3 * thin + 2 * part), axis=0
+    )
+    tall_sum = jnp.sum(tall_back.astype(jnp.float32), axis=0)
+    in_grad = (
+        wide_sum[:, :, : 3 * thin]
+        .reshape(team, depth, 3, thin)
+        .transpose(1, 2, 0, 3)
+        .reshape(in_weight.shape)
+    )
+    gate_out = wide_sum[:, :, 3 * thin : 3 * thin + part].transpose(1, 0, 2).reshape(depth, inner)
+    up_out = wide_sum[:, :, 3 * thin + part :].transpose(1, 0, 2).reshape(depth, inner)
+    gain_one_grad, kernel_grad, gain_two_grad = lax.psum(
+        (gain_one_local, kernel_local, gain_two_local), "row"
+    )
+    return (
+        block_out,
+        tokens_grad,
+        gain_one_grad,
+        in_grad,
+        kernel_grad,
+        tall_sum[:depth],
+        gain_two_grad,
+        gate_out,
+        up_out,
+        tall_sum[depth:],
+    )
+
+
 def solution(mesh):
     in_specs = (
         P("row", "col"),
@@ -193,4 +632,7 @@
         P("row", "col"),
         P("row", "col"),
     )
-    return jax.shard_map(local, mesh=mesh, in_specs=in_specs, out_specs=out_specs, check_vma=False)
+    rows, cols = mesh.shape["row"], mesh.shape["col"]
+    shared = cols > 1 and rows % cols == 0 and rows // cols > 1
+    body = teams if shared else local
+    return jax.shard_map(body, mesh=mesh, in_specs=in_specs, out_specs=out_specs, check_vma=False)

time: 1150 us -> 417 us (0.36)
  waiting for transfers between devices: 963 us -> 5 us
  Pallas kernels: 0 us -> 246 us
  matrix products: 50.1 us -> 23.5 us
  starting transfers between devices: 5.37 us -> 21.1 us
  between operations: 14.3 us -> 1.24 us
  local copies, waits for them, and re-layouts: 8.6 us -> 21.6 us
    reduce_scatter x8 -> x0, waiting for transfers between devices: 609 us -> none  [the longest x4 585 us: weight_terms(): lax.psum_scatter(jnp.einsum('tr,tkc->rkc', left, grad, preferred_element_...]
    all_gather x6 -> x0, waiting for transfers between devices: 345 us -> none  [the longest x1 83.4 us: local(): lax.all_gather(down_weight, 'row', axis=0, tiled=True)]
    pallas_call x0 -> x9, Pallas kernels: none -> 246 us  [the longest x2 92.4 us: exchange(): pl.pallas_call(functools.partial(exchange_kernel, team, cols, outward), o...]
    dot_general x12, matrix products: 50.1 us -> 23.5 us  [dot(): lax.dot_general(a, b, (((a_dim,), (b_dim,)), ((), ())), preferred_element...]
    ppermute x2, starting transfers between devices: 4.63 us -> 21.1 us  [shifted(): return lax.ppermute(block, axis, route)]
  transfers between devices with their start and end apart: 16 -> 2, of which waited for: 14 -> 2; matrix products, arithmetic and copies ran while one was open for 5% -> 1% of each run, Pallas kernels for 0% -> 0%
where the time goes in v1:
time: 417 us
  Pallas kernels  246 us (59%)
  blocking collectives  86.1 us (21%)
  matrix products  23.5 us (6%)
  local copies, waits for them, and re-layouts  21.6 us (5%)
  starting transfers between devices  21.1 us (5%)
  other arithmetic  12 us (3%)
  waiting for transfers between devices  5 us (1%)
    pallas_call x2, Pallas kernels, exchange(): pl.pallas_call(functools.partial(exchange_kernel, team, cols, outward), o...  92.4 us
    pallas_call x4, Pallas kernels, scatter(): pl.pallas_call(functools.partial(scatter_kernel, team, cols), out_shape=j...  81.6 us
    psum x1, blocking collectives, teams(): lax.psum((gain_one_local, kernel_local, gain_two_local), 'row')  75.9 us
    pallas_call x3, Pallas kernels, gather(): pl.pallas_call(functools.partial(gather_kernel, team, cols, count), out_s...  72.3 us
    dot_general x12, matrix products, dot(): lax.dot_general(a, b, (((a_dim,), (b_dim,)), ((), ())), preferred_element...  23.5 us
    ppermute x2, starting transfers between devices, shifted(): return lax.ppermute(block, axis, route)  21.1 us
  transfers between devices with their start and end apart: 2, of which 2 were waited for; matrix products, arithmetic and copies ran while one was open for 1% of the time, Pallas kernels for 0%

profile of v1, /device:TPU:0, one launch (start us, length us, event | category | flops | bytes accessed | tf_op | source)
XLA Modules:
  0.0 416.8 jit_solution(15741408803452944180)
XLA Ops:
  1.7 2.6 psum.49
  5.6 1.6 reshape.82
  7.2 1.6 reshape.83
  10.3 34.6 %shard_map.186 = (bf16[1024,1024]{1,0:T(8,128)(2,1)}, bf16[1024,1024]{1,0:T(8,128)(2,1)}) custom-call(bf16[128,512]{1,0:T(8,128)(2,1)} %fusion.15.refs_0_, bf16[128,512]{1,0:T(8,128)(2,1)} %refs_1_.1), custom_call_target="tpu_custom_call" | custom-call | tf_op jit(solution)/shard_map/pallas_call | solution.py:263
  47.2 38.7 %shard_map.187 = (bf16[16,64,768]{2,1,0:T(8,128)(2,1)}, bf16[2,352,512]{2,1,0:T(8,128)(2,1)}) custom-call(bf16[8,64,768]{2,1,0:T(8,128)(2,1)} %pad_maximum_fusion.2.wide_ref, bf16[352,512]{1,0:T(8,128)(2,1)} %pad_maximum_fusion.7.tall_ref), custom_call_target="tpu_custom_call" | custom-call | tf_op jit(solution)/shard_map/pallas_call | solution.py:428
  85.9 2.6 fusion.5
  88.6 19.6 %collective-permute-start = (f32[2,64]{0,1:T(8,128)S(1)}, f32[2,64]{0,1:T(8,128)S(1)}, u32[]{:S(2)}, u32[]{:S(2)}) collective-permute-start(f32[2,64]{0,1:T(8,128)S(1)} %slice.127), channel_id=1, source_target_pairs={{0,16},{2,18},{4,20},{6,22},{8,24},{10,26},{12,28},{14,30},{1,17},... | collective-permute-start | bytes 1544 | tf_op jit(solution)/shard_map/ppermute | solution.py:19
  110.8 20.7 %shard_map.188 = f32[128,512]{1,0:T(8,128)S(1)} custom-call(bf16[1024,1024]{1,0:T(8,128)(2,1)S(1)} %convolution_convert_fusion.2.x_ref), custom_call_target="tpu_custom_call" | custom-call | tf_op jit(solution)/shard_map/pallas_call | solution.py:334
  131.5 2.6 psum.50
  135.0 18.3 %shard_map.189 = bf16[1024,1024]{1,0:T(8,128)(2,1)} custom-call(bf16[128,512]{1,0:T(8,128)(2,1)} %multiply_convert_fusion.6.refs_0_), custom_call_target="tpu_custom_call" | custom-call | tf_op jit(solution)/shard_map/pallas_call | solution.py:263
  153.3 4.1 fusion.2
  160.8 20.1 %shard_map.190 = f32[128,512]{1,0:T(8,128)S(1)} custom-call(bf16[1024,1024]{1,0:T(8,128)(2,1)S(1)} %convolution_convert_fusion.1.x_ref), custom_call_target="tpu_custom_call" | custom-call | tf_op jit(solution)/shard_map/pallas_call | solution.py:334
  181.0 2.2 convolution_convert_fusion.3.x_ref
  183.1 19.9 %shard_map.191 = f32[128,512]{1,0:T(8,128)S(1)} custom-call(bf16[1024,1024]{1,0:T(8,128)(2,1)S(1)} %convolution_convert_fusion.3.x_ref), custom_call_target="tpu_custom_call" | custom-call | tf_op jit(solution)/shard_map/pallas_call | solution.py:334
  203.2 2.5 psum.51
  206.7 19.3 %shard_map.192 = bf16[1024,1024]{1,0:T(8,128)(2,1)} custom-call(bf16[128,512]{1,0:T(8,128)(2,1)} %get-tuple-element.55.refs_0_), custom_call_target="tpu_custom_call" | custom-call | tf_op jit(solution)/shard_map/pallas_call | solution.py:263
  226.0 2.2 convolution_convert_fusion.7
  229.9 3.5 convolution_convert_fusion.4
  233.7 1.5 collective-permute-start.1
  236.3 4.6 %collective-permute-done.1 = f32[2,64]{0,1:T(8,128)S(1)} collective-permute-done((f32[2,64]{0,1:T(8,128)S(1)}, f32[2,64]{0,1:T(8,128)S(1)}, u32[]{:S(2)}, u32[]{:S(2)}) %collective-permute-start.1) | collective-permute-done | bytes 544 | tf_op jit(solution)/shard_map/ppermute | solution.py:19
  241.2 2.3 convolution_convert_fusion.6
  243.6 1.6 copy.61
  245.2 53.7 %shard_map.194 = (bf16[16,64,768]{2,1,0:T(8,128)(2,1)}, bf16[2,352,512]{2,1,0:T(8,128)(2,1)}) custom-call(bf16[16,64,768]{2,1,0:T(8,128)(2,1)} %bitcast.63, bf16[2,352,512]{2,1,0:T(8,128)(2,1)} %bitcast.66), custom_call_target="tpu_custom_call" | custom-call | tf_op jit(solution)/shard_map/pallas_call | solution.py:428
  298.9 1.9 convert_reduce_fusion
  304.1 1.8 convolution_convert_fusion.x_ref
  305.9 1.3 copy.65
  307.3 2.2 reshape.91
  310.8 2.2 reshape.92
  314.4 2.1 reshape.90
  316.5 20.9 %shard_map.193 = f32[128,512]{1,0:T(8,128)S(1)} custom-call(bf16[1024,1024]{1,0:T(8,128)(2,1)S(1)} %convolution_convert_fusion.x_ref), custom_call_target="tpu_custom_call" | custom-call | tf_op jit(solution)/shard_map/pallas_call | solution.py:334
  337.6 2.5 psum.52
  340.1 75.9 %all-reduce = (f32[512]{0:T(512)}, f32[3,512]{1,0:T(4,128)}, f32[512]{0:T(512)}) all-reduce(f32[512]{0:T(512)S(1)} %get-tuple-element.47, f32[3,512]{1,0:T(4,128)S(1)} %dynamic_update_slice.3, f32[512]{0:T(512)S(1)} %get-tuple-element.44), channel_id=1, replica_groups=mesh['row'=16,'col'=2] {'row'}, use_global_device_ids=true, to_apply=%region_9.0 | all-reduce | flops 2560 | bytes 20480 | tf_op jit(solution)/shard_map/psum | solution.py:592
  (102 shorter events, 24.5 us)
Async XLA Ops:
  0.6 8.1 %copy-start.11 = (bf16[64,3,512]{2,0,1:T(8,128)(2,1)S(1)}, bf16[64,3,512]{2,0,1:T(8,128)(2,1)}, u32[]{:S(2)}) copy-start(bf16[64,3,512]{2,0,1:T(8,128)(2,1)} %param.14) | copy-start | bytes 589828
  4.9 4.7 %copy-start.14 = (f32[128]{0:T(128)}, f32[128]{0:T(128)S(1)}, u32[]{:S(2)}) copy-start(f32[128]{0:T(128)S(1)} %get-tuple-element.76) | copy-start | bytes 1540
  5.6 4.0 copy-start.2
  9.3 35.8 %copy-start.10 = (bf16[288,512]{1,0:T(8,128)(2,1)S(1)}, bf16[288,512]{1,0:T(8,128)(2,1)}, u32[]{:S(2)}) copy-start(bf16[288,512]{1,0:T(8,128)(2,1)} %param.20) | copy-start | bytes 884740
  9.3 35.8 %copy-start.12 = (bf16[64,512]{1,0:T(8,128)(2,1)S(1)}, bf16[64,512]{1,0:T(8,128)(2,1)}, u32[]{:S(2)}) copy-start(bf16[64,512]{1,0:T(8,128)(2,1)} %param.16) | copy-start | bytes 196612
  85.9 22.3 %copy-start.6 = (bf16[2,352,512]{2,1,0:T(8,128)(2,1)S(1)}, bf16[2,352,512]{2,1,0:T(8,128)(2,1)}, u32[]{:S(2)}) copy-start(bf16[2,352,512]{2,1,0:T(8,128)(2,1)} %get-tuple-element.18) | copy-start | bytes 2162692
  88.5 20.6 %copy-start.13 = (s32[2048]{0:T(1024)S(1)}, s32[2048]{0:T(1024)}, u32[]{:S(2)}) copy-start(s32[2048]{0:T(1024)} %param.12) | copy-start | bytes 24580
  88.5 20.7 %copy-start.16 = (bf16[512]{0:T(512)(128)(2,1)S(1)}, bf16[512]{0:T(512)(128)(2,1)}, u32[]{:S(2)}) copy-start(bf16[512]{0:T(512)(128)(2,1)} %param.17) | copy-start | bytes 3076
  88.6 21.1 %collective-permute-start = (f32[2,64]{0,1:T(8,128)S(1)}, f32[2,64]{0,1:T(8,128)S(1)}, u32[]{:S(2)}, u32[]{:S(2)}) collective-permute-start(f32[2,64]{0,1:T(8,128)S(1)} %slice.127), channel_id=1, source_target_pairs={{0,16},{2,18},{4,20},{6,22},{8,24},{10,26},{12,28},{14,30},{1,17},... | collective-permute-start | bytes 1544 | tf_op jit(solution)/shard_map/ppermute | solution.py:19
  153.3 4.1 copy-start.18
  158.7 22.2 %copy-start.19 = (bf16[1024,288]{0,1:T(8,128)(2,1)}, bf16[1024,288]{0,1:T(8,128)(2,1)S(1)}, u32[]{:S(2)}) copy-start(bf16[1024,288]{0,1:T(8,128)(2,1)S(1)} %get-tuple-element.61) | copy-start | bytes 1769476
  158.7 22.2 %copy-start.21 = (bf16[1024,288]{0,1:T(8,128)(2,1)}, bf16[1024,288]{0,1:T(8,128)(2,1)S(1)}, u32[]{:S(2)}) copy-start(bf16[1024,288]{0,1:T(8,128)(2,1)S(1)} %get-tuple-element.62) | copy-start | bytes 1769476
  160.8 20.1 %copy-start.8 = (bf16[16,64,768]{2,1,0:T(8,128)(2,1)S(1)}, bf16[16,64,768]{2,1,0:T(8,128)(2,1)}, u32[]{:S(2)}) copy-start(bf16[16,64,768]{2,1,0:T(8,128)(2,1)} %get-tuple-element.17) | copy-start | bytes 4718596
  183.1 22.6 %copy-start.9 = (bf16[128,512]{1,0:T(8,128)(2,1)S(1)}, bf16[128,512]{1,0:T(8,128)(2,1)}, u32[]{:S(2)}) copy-start(bf16[128,512]{1,0:T(8,128)(2,1)} %refs_1_.1) | copy-start | bytes 393220
  226.0 2.3 copy-start
  226.0 3.0 copy-start.20
  228.3 1.6 copy-start.3
  233.7 7.2 %collective-permute-start.1 = (f32[2,64]{0,1:T(8,128)S(1)}, f32[2,64]{0,1:T(8,128)S(1)}, u32[]{:S(2)}, u32[]{:S(2)}) collective-permute-start(f32[2,64]{0,1:T(8,128)S(1)} %slice.135), channel_id=1, source_target_pairs={{16,0},{18,2},{20,4},{22,6},{24,8},{26,10},{28,12},{30,14},{17,1},... | collective-permute-start | bytes 1544 | tf_op jit(solution)/shard_map/ppermute | solution.py:19
  241.2 2.3 copy-start.4
  300.8 1.2 copy-start.1
  300.8 1.6 copy-start.7
  309.4 3.5 slice-start
  314.4 23.0 %copy-start.15 = (f32[128]{0:T(128)S(1)}, f32[128]{0:T(128)}, u32[]{:S(2)}) copy-start(f32[128]{0:T(128)} %copy-done.14) | copy-start | bytes 1540
  316.5 99.5 %copy-start.5 = (f32[128,512]{1,0:T(8,128)S(1)}, f32[128,512]{1,0:T(8,128)}, u32[]{:S(2)}) copy-start(f32[128,512]{1,0:T(8,128)} %get-tuple-element.56) | copy-start | bytes 786436
  316.5 99.5 %copy-start.17 = (f32[128]{0:T(128)S(1)}, f32[128]{0:T(128)}, u32[]{:S(2)}) copy-start(f32[128]{0:T(128)} %get-tuple-element.75) | copy-start | bytes 1540

commit v2 on v0

--- a/solution.py
+++ b/solution.py
@@ -1,6 +1,10 @@
+import functools
+
 import jax
 import jax.numpy as jnp
 from jax import lax
+from jax.experimental import pallas as pl
+from jax.experimental.pallas import tpu as pltpu
 from jax.sharding import PartitionSpec as P
 
 D = 1024
@@ -167,6 +171,593 @@
     )
 
 
+MESH = pl.DeviceIdType.MESH
+VMEM = pl.BlockSpec(memory_space=pltpu.VMEM)
+ANY = pl.BlockSpec(memory_space=pl.ANY)
+
+
+def greet(devices):
+    barrier = pltpu.get_barrier_semaphore()
+    for device in devices:
+        pl.semaphore_signal(barrier, inc=1, device_id=device, device_id_type=MESH)
+    pl.semaphore_wait(barrier, len(devices))
+
+
+def remote(source, target, send, receive, device):
+    return pltpu.make_async_remote_copy(
+        src_ref=source,
+        dst_ref=target,
+        send_sem=send,
+        recv_sem=receive,
+        device_id=device,
+        device_id_type=MESH,
+    )
+
+
+class Here:
+    def __init__(self, team, cols):
+        self.team, self.cols, self.rows = team, cols, team * cols
+        self.row, self.col = lax.axis_index("row"), lax.axis_index("col")
+        self.place, self.group = lax.rem(self.row, team), lax.div(self.row, team)
+        first = self.row - self.place
+        self.mates = [None] + [first + lax.rem(self.place + k, team) for k in range(1, team)]
+        self.others = [None] + [lax.rem(self.col + j, cols) for j in range(1, cols)]
+        self.peers = [None] + [lax.rem(self.row + k, self.rows) for k in range(1, self.rows)]
+
+    def greet(self):
+        devices = [(peer, self.col) for peer in self.peers[1:]]
+        for m in range(self.cols):
+            there = lax.rem(self.group + m, self.cols) * self.team + self.place
+            devices += [(there, other) for other in self.others[1:]]
+        barrier = pltpu.get_barrier_semaphore()
+        for device in devices:
+            pl.semaphore_signal(barrier, inc=1, device_id=device, device_id_type=MESH)
+        pl.semaphore_wait(barrier, len(devices))
+
+
+class Gather:
+    def __init__(self, block, team, cols):
+        self.operands, self.in_specs, self.out_specs = [block], [ANY], [ANY]
+        tall, wide = block.shape
+        self.out_shape = [jax.ShapeDtypeStruct((tall * team, wide * cols), block.dtype)]
+        self.scratch = [
+            pltpu.SemaphoreType.DMA((team,)),
+            pltpu.SemaphoreType.DMA((team,)),
+            pltpu.SemaphoreType.DMA((team, cols)),
+            pltpu.SemaphoreType.DMA((team, cols)),
+            pltpu.SemaphoreType.DMA((1,)),
+        ]
+
+    def bind(self, here, x_ref, o_ref, send, recv, pass_send, pass_recv, own):
+        self.here, self.x_ref, self.o_ref = here, x_ref, o_ref
+        self.send, self.recv = send, recv
+        self.pass_send, self.pass_recv, self.own = pass_send, pass_recv, own
+
+    def slot(self, k, side):
+        tall, wide = self.x_ref.shape
+        origin = lax.rem(self.here.place - k + self.here.team, self.here.team)
+        return self.o_ref.at[
+            pl.ds(pl.multiple_of(origin * tall, tall), tall),
+            pl.ds(pl.multiple_of(side * wide, wide), wide),
+        ]
+
+    def row_copy(self, source, target, k):
+        device = (self.here.mates[k], self.here.col)
+        return remote(source, target, self.send.at[k], self.recv.at[k], device)
+
+    def col_copy(self, source, target, k, j):
+        device = (self.here.row, self.here.others[j])
+        return remote(source, target, self.pass_send.at[k, j], self.pass_recv.at[k, j], device)
+
+    def start(self):
+        here = self.here
+        mine = self.slot(0, here.col)
+        self.sends = [self.row_copy(self.x_ref, mine, k) for k in range(1, here.team)]
+        self.passes = [self.col_copy(self.x_ref, mine, 0, j) for j in range(1, here.cols)]
+        self.mine = pltpu.make_async_copy(self.x_ref, mine, self.own.at[0])
+        for copy in self.sends + self.passes + [self.mine]:
+            copy.start()
+
+    def middle(self):
+        here = self.here
+        for k in range(1, here.team):
+            arrived = self.slot(k, here.col)
+            self.row_copy(arrived, arrived, k).wait_recv()
+            for j in range(1, here.cols):
+                copy = self.col_copy(arrived, arrived, k, j)
+                copy.start()
+                self.passes.append(copy)
+
+    def finish(self):
+        here = self.here
+        for k in range(here.team):
+            for j in range(1, here.cols):
+                landed = self.slot(k, lax.rem(here.col - j + here.cols, here.cols))
+                self.col_copy(landed, landed, k, j).wait_recv()
+        for copy in self.passes + self.sends:
+            copy.wait_send()
+        self.mine.wait()
+
+
+class Scatter:
+    def __init__(self, partial_sum, team, cols):
+        self.operands, self.in_specs, self.out_specs = [partial_sum], [VMEM], [VMEM]
+        tall, wide = partial_sum.shape[0] // team, partial_sum.shape[1] // cols
+        self.out_shape = [jax.ShapeDtypeStruct((tall, wide), jnp.float32)]
+        self.scratch = [
+            pltpu.VMEM((cols - 1, team, tall, wide), jnp.bfloat16),
+            pltpu.VMEM((team - 1, tall, wide), jnp.bfloat16),
+            pltpu.VMEM((team - 1, tall, wide), jnp.bfloat16),
+            pltpu.SemaphoreType.DMA((team,)),
+            pltpu.SemaphoreType.DMA((team,)),
+            pltpu.SemaphoreType.DMA((team, cols)),
+            pltpu.SemaphoreType.DMA((team, cols)),
+        ]
+
+    def bind(self, here, x_ref, o_ref, inbox, stage, land, send, recv, pass_send, pass_recv):
+        self.here, self.x_ref, self.o_ref = here, x_ref, o_ref
+        self.inbox, self.stage, self.land = inbox, stage, land
+        self.send, self.recv = send, recv
+        self.pass_send, self.pass_recv = pass_send, pass_recv
+
+    def part(self, k, side):
+        tall, wide = self.o_ref.shape
+        origin = lax.rem(self.here.place + k, self.here.team)
+        return self.x_ref.at[
+            pl.ds(pl.multiple_of(origin * tall, tall), tall),
+            pl.ds(pl.multiple_of(side * wide, wide), wide),
+        ]
+
+    def start(self):
+        here = self.here
+        self.order = list(range(1, here.team)) + [0]
+        self.passes, self.sends = {}, {}
+        for k in self.order:
+            for j in range(1, here.cols):
+                self.passes[k, j] = remote(
+                    self.part(k, here.others[j]),
+                    self.inbox.at[j - 1, k],
+                    self.pass_send.at[k, j],
+                    self.pass_recv.at[k, j],
+                    (here.row, here.others[j]),
+                )
+                self.passes[k, j].start()
+
+    def middle(self):
+        here = self.here
+        for k in self.order:
+            total = self.part(k, here.col)[...].astype(jnp.float32)
+            for j in range(1, here.cols):
+                self.passes[k, j].wait_recv()
+                total = total + self.inbox[j - 1, k].astype(jnp.float32)
+            if k:
+                self.stage[k - 1] = total.astype(jnp.bfloat16)
+                self.sends[k] = remote(
+                    self.stage.at[k - 1],
+                    self.land.at[k - 1],
+                    self.send.at[k],
+                    self.recv.at[k],
+                    (here.mates[k], here.col),
+                )
+                self.sends[k].start()
+            else:
+                self.o_ref[...] = total
+
+    def finish(self):
+        for k in self.sends:
+            self.sends[k].wait_recv()
+            self.o_ref[...] += self.land[k - 1].astype(jnp.float32)
+        for copy in list(self.passes.values()) + list(self.sends.values()):
+            copy.wait_send()
+
+
+class Wide:
+    def __init__(self, blocks, team, cols, outward):
+        rows = team * cols
+        self.outward = outward
+        self.operands, self.in_specs, self.out_specs = [blocks], [ANY], [ANY]
+        self.out_shape = [jax.ShapeDtypeStruct((rows,) + blocks.shape[1:], blocks.dtype)]
+        self.scratch = [
+            pltpu.SemaphoreType.DMA((rows,)),
+            pltpu.SemaphoreType.DMA((rows,)),
+            pltpu.SemaphoreType.DMA((1,)),
+        ]
+
+    def bind(self, here, x_ref, o_ref, send, recv, own):
+        self.here, self.x_ref, self.o_ref = here, x_ref, o_ref
+        self.send, self.recv, self.own = send, recv, own
+
+    def source(self, peer):
+        return self.x_ref.at[lax.rem(peer, self.here.team) if self.outward else peer]
+
+    def copy(self, source, target, k):
+        device = (self.here.peers[k], self.here.col)
+        return remote(source, target, self.send.at[k], self.recv.at[k], device)
+
+    def start(self):
+        here = self.here
+        mine = self.o_ref.at[here.row]
+        self.copies = [
+            self.copy(self.source(here.peers[k]), mine, k) for k in range(1, here.rows)
+        ]
+        self.mine = pltpu.make_async_copy(self.source(here.row), mine, self.own.at[0])
+        for copy in self.copies + [self.mine]:
+            copy.start()
+
+    def middle(self):
+        pass
+
+    def finish(self):
+        here = self.here
+        for k in range(1, here.rows):
+            landed = self.o_ref.at[lax.rem(here.row - k + here.rows, here.rows)]
+            self.copy(landed, landed, k).wait_recv()
+        for copy in self.copies:
+            copy.wait_send()
+        self.mine.wait()
+
+
+class Tall:
+    def __init__(self, block, team, cols, outward):
+        self.outward = outward
+        self.operands, self.in_specs, self.out_specs = [block], [ANY], [ANY]
+        self.out_shape = [jax.ShapeDtypeStruct((cols,) + block.shape[-2:], block.dtype)]
+        self.scratch = [
+            pltpu.SemaphoreType.DMA((cols,)),
+            pltpu.SemaphoreType.DMA((cols,)),
+            pltpu.SemaphoreType.DMA((1,)),
+        ]
+
+    def bind(self, here, x_ref, o_ref, send, recv, own):
+        self.here, self.x_ref, self.o_ref = here, x_ref, o_ref
+        self.send, self.recv, self.own = send, recv, own
+        self.home = here.group == here.col
+
+    def target(self, m):
+        here = self.here
+        if self.outward:
+            return lax.rem(here.group + m, here.cols) * here.team + here.place, here.group
+        return here.col * here.team + here.place, lax.rem(here.col + m, here.cols)
+
+    def copy(self, m):
+        here = self.here
+        if self.outward:
+            source, index = self.x_ref, here.col
+        else:
+            source, index = self.x_ref.at[lax.rem(here.col + m, here.cols)], here.group
+        return remote(
+            source, self.o_ref.at[index], self.send.at[m], self.recv.at[index], self.target(m)
+        )
+
+    def mine(self):
+        source = self.x_ref if self.outward else self.x_ref.at[self.here.col]
+        return pltpu.make_async_copy(source, self.o_ref.at[self.here.col], self.own.at[0])
+
+    def start(self):
+        for m in range(1, self.here.cols):
+            self.copy(m).start()
+        pl.when(self.home)(lambda: self.mine().start())
+        pl.when(jnp.logical_not(self.home))(lambda: self.copy(0).start())
+
+    def middle(self):
+        pass
+
+    def finish(self):
+        here = self.here
+        for j in range(here.cols):
+            landed = self.o_ref.at[j]
+            arriving = remote(landed, landed, self.send.at[0], self.recv.at[j], self.target(1))
+            own = jnp.logical_and(self.home, here.col == j)
+            pl.when(own)(lambda: self.mine().wait())
+            pl.when(jnp.logical_not(own))(lambda arriving=arriving: arriving.wait_recv())
+        for m in range(1, here.cols):
+            self.copy(m).wait_send()
+        pl.when(jnp.logical_not(self.home))(lambda: self.copy(0).wait_send())
+
+
+class Totals:
+    def __init__(self, few, factor, scattered, rows):
+        self.scattered = scattered
+        self.operands, self.in_specs, self.out_specs = [few, factor], [VMEM, VMEM], [VMEM]
+        self.out_shape = [jax.ShapeDtypeStruct(few.shape, few.dtype)]
+        self.scratch = [
+            pltpu.VMEM(few.shape, few.dtype),
+            pltpu.VMEM((rows,) + few.shape, few.dtype),
+            pltpu.SemaphoreType.DMA((rows,)),
+            pltpu.SemaphoreType.DMA((rows,)),
+        ]
+
+    def bind(self, here, few_ref, factor_ref, o_ref, out_box, land, send, recv):
+        self.here, self.few_ref, self.factor_ref, self.o_ref = here, few_ref, factor_ref, o_ref
+        self.out_box, self.land, self.send, self.recv = out_box, land, send, recv
+
+    def start(self):
+        pass
+
+    def middle(self):
+        pass
+
+    def copy(self, source, target, k):
+        device = (self.here.peers[k], self.here.col)
+        return remote(source, target, self.send.at[k], self.recv.at[k], device)
+
+    def finish(self):
+        here = self.here
+        last = self.few_ref.shape[0] - 1
+        made = jnp.sum(self.scattered.o_ref[...] * self.factor_ref[...], axis=0, keepdims=True)
+        self.out_box[...] = self.few_ref[...]
+        self.out_box[last:] = made
+        copies = [
+            self.copy(self.out_box, self.land.at[here.row], k) for k in range(1, here.rows)
+        ]
+        for copy in copies:
+            copy.start()
+        self.land[here.row] = self.out_box[...]
+        for k in range(1, here.rows):
+            landed = self.land.at[lax.rem(here.row - k + here.rows, here.rows)]
+            self.copy(landed, landed, k).wait_recv()
+        total = self.land[0]
+        for k in range(1, here.rows):
+            total = total + self.land[k]
+        self.o_ref[...] = total
+        for copy in copies:
+            copy.wait_send()
+
+
+def together_kernel(team, cols, parts, *refs):
+    here = Here(team, cols)
+    refs = list(refs)
+
+    def take(counts):
+        return [[refs.pop(0) for _ in range(count)] for count in counts]
+
+    ins = take([len(part.operands) for part in parts])
+    outs = take([len(part.out_shape) for part in parts])
+    scratch = take([len(part.scratch) for part in parts])
+    for part, a, b, c in zip(parts, ins, outs, scratch):
+        part.bind(here, *a, *b, *c)
+    here.greet()
+    for part in parts:
+        part.start()
+    for part in parts:
+        part.middle()
+    for part in parts:
+        part.finish()
+
+
+def together(identity, team, cols, *parts):
+    return pl.pallas_call(
+        functools.partial(together_kernel, team, cols, parts),
+        out_shape=[shape for part in parts for shape in part.out_shape],
+        in_specs=[spec for part in parts for spec in part.in_specs],
+        out_specs=[spec for part in parts for spec in part.out_specs],
+        scratch_shapes=[shape for part in parts for shape in part.scratch],
+        compiler_params=pltpu.CompilerParams(
+            collective_id=identity, has_side_effects=True, vmem_limit_bytes=32 * 2**20
+        ),
+    )(*[operand for part in parts for operand in part.operands])
+
+
+def dot(a, b, a_dim, b_dim, kind=jnp.float32):
+    out = lax.dot_general(
+        a, b, (((a_dim,), (b_dim,)), ((), ())), preferred_element_type=jnp.float32
+    )
+    return out.astype(kind)
+
+
+def cuts(whole):
+    first, second = whole // 384 * 128, whole // 192 * 128
+    return ((0, first), (first, second), (second, whole))
+
+
+def teams(
+    tokens,
+    segments,
+    first_gain,
+    in_weight,
+    conv_kernel,
+    out_weight,
+    second_gain,
+    gate_weight,
+    up_weight,
+    down_weight,
+    cotangent,
+):
+    bf = jnp.bfloat16
+    rows, cols = lax.axis_size("row"), lax.axis_size("col")
+    team = rows // cols
+    row, col = lax.axis_index("row"), lax.axis_index("col")
+    place, group = lax.rem(row, team), lax.div(row, team)
+    depth, _, width = in_weight.shape
+    inner = gate_weight.shape[1]
+    thin, part = width // team, inner // team
+    held = tokens.shape[0] * team
+    blocks = in_weight.reshape(depth, 3, team, thin).transpose(2, 0, 1, 3)
+    wide = jnp.concatenate(
+        [
+            blocks.reshape(team, depth, 3 * thin),
+            gate_weight.reshape(depth, team, part).transpose(1, 0, 2),
+            up_weight.reshape(depth, team, part).transpose(1, 0, 2),
+        ],
+        axis=2,
+    )
+    pieces = [wide[:, :, start:stop] for start, stop in cuts(wide.shape[2])]
+    tok_float = tokens.astype(jnp.float32)
+    gain_one = first_gain.astype(jnp.float32)
+    gain_two = second_gain.astype(jnp.float32)
+    kernel = lax.dynamic_slice_in_dim(conv_kernel, place * thin, thin, 1).astype(jnp.float32)
+    inv_one = squares_inverse(tok_float)
+    normed_one = (tok_float * inv_one * gain_one).astype(bf)
+
+    normed_full, first_wide, out_blocks = together(
+        1,
+        team,
+        cols,
+        Gather(normed_one, team, cols),
+        Wide(pieces[0], team, cols, True),
+        Tall(out_weight, team, cols, True),
+    )
+    first_wide = first_wide.reshape(rows * depth, -1)
+    in_part = first_wide[:, : 3 * thin]
+    out_part = out_blocks.transpose(1, 0, 2).reshape(depth, cols * width)
+
+    projected = dot(normed_full, in_part, 1, 0)
+    b_part = projected[:, :thin]
+    c_part = projected[:, thin : 2 * thin]
+    x_part = projected[:, 2 * thin :]
+    gated = b_part * x_part
+    padded = jnp.concatenate(
+        [jnp.full((2,), -1, jnp.int32), segments, jnp.full((2,), -2, jnp.int32)]
+    )
+    window = lax.dynamic_slice_in_dim(padded, group * held, held + 4)
+    own_ids = window[2 : held + 2]
+    same_one = (own_ids == window[1 : held + 1]).astype(jnp.float32)[:, None]
+    same_two = (own_ids == window[0:held]).astype(jnp.float32)[:, None]
+    after_one = (window[3 : held + 3] == own_ids).astype(jnp.float32)[:, None]
+    after_two = (window[4 : held + 4] == own_ids).astype(jnp.float32)[:, None]
+    earlier = shifted(gated[held - 2 :], "row", team)
+    extended = jnp.concatenate([earlier, gated], axis=0)
+    back_one = extended[1 : held + 1] * same_one
+    back_two = extended[0:held] * same_two
+    mixed = kernel[0] * gated + kernel[1] * back_one + kernel[2] * back_two
+    conv_out = (c_part * mixed).astype(bf)
+    attended, cot_full, second_wide = together(
+        2,
+        team,
+        cols,
+        Scatter(dot(conv_out, out_part, 1, 0, bf), team, cols),
+        Gather(cotangent, team, cols),
+        Wide(pieces[1], team, cols, True),
+    )
+    middle = tok_float + attended
+    inv_two = squares_inverse(middle)
+    normed_two = (middle * inv_two * gain_two).astype(bf)
+    two_full, third_wide, down_blocks = together(
+        3,
+        team,
+        cols,
+        Gather(normed_two, team, cols),
+        Wide(pieces[2], team, cols, True),
+        Tall(down_weight, team, cols, True),
+    )
+    down_part = down_blocks.transpose(1, 0, 2).reshape(part, cols * width)
+    pair_part = jnp.concatenate(
+        [
+            first_wide[:, 3 * thin :],
+            second_wide.reshape(rows * depth, -1),
+            third_wide.reshape(rows * depth, -1),
+        ],
+        axis=1,
+    )
+    both = dot(two_full, pair_part, 1, 0)
+    gate_value, up_value = both[:, :part], both[:, part:]
+    sigma = jax.nn.sigmoid(gate_value)
+    activated = gate_value * sigma
+    hidden = (activated * up_value).astype(bf)
+    hidden_grad = dot(cot_full, down_part, 1, 1)
+    gate_grad = hidden_grad * up_value * sigma * (1.0 + gate_value * (1.0 - sigma))
+    up_grad = hidden_grad * activated
+    pair_grad = jnp.concatenate([gate_grad.astype(bf), up_grad.astype(bf)], axis=1)
+    edges = cuts(3 * thin + 2 * part)
+    pair_weight_grad = dot(two_full, pair_grad, 0, 0, bf)
+    grad_pieces = [
+        pair_weight_grad[:, max(start - 3 * thin, 0) : stop - 3 * thin].reshape(rows, depth, -1)
+        for start, stop in edges
+    ]
+    down_grad = dot(hidden, cot_full, 0, 0, bf)
+    normed_two_grad, third_back, down_back = together(
+        4,
+        team,
+        cols,
+        Scatter(dot(pair_grad, pair_part, 1, 1, bf), team, cols),
+        Wide(grad_pieces[2], team, cols, False),
+        Tall(down_grad.reshape(part, cols, width).transpose(1, 0, 2), team, cols, False),
+    )
+    middle_back, gain_two_local = norm_backward(normed_two_grad, gain_two, middle, inv_two)
+    middle_grad = cotangent.astype(jnp.float32) + middle_back
+    branch_out, attended_grad, second_back = together(
+        5,
+        team,
+        cols,
+        Scatter(dot(hidden, down_part, 1, 0, bf), team, cols),
+        Gather(middle_grad.astype(bf), team, cols),
+        Wide(grad_pieces[1], team, cols, False),
+    )
+    block_out = (middle + branch_out).astype(bf)
+    conv_grad = dot(attended_grad, out_part, 1, 1)
+    c_grad = conv_grad * mixed
+    mixed_grad = conv_grad * c_part
+    later = shifted(mixed_grad[0:2], "row", -team)
+    ahead = jnp.concatenate([mixed_grad, later], axis=0)
+    gated_grad = (
+        kernel[0] * mixed_grad
+        + kernel[1] * after_one * ahead[1 : held + 1]
+        + kernel[2] * after_two * ahead[2 : held + 2]
+    )
+    kernel_local = jnp.stack(
+        [
+            jnp.sum(mixed_grad * gated, axis=0),
+            jnp.sum(mixed_grad * back_one, axis=0),
+            jnp.sum(mixed_grad * back_two, axis=0),
+        ]
+    )
+    kernel_local = lax.dynamic_update_slice_in_dim(
+        jnp.zeros((3, width), jnp.float32), kernel_local, place * thin, 1
+    )
+    projected_grad = jnp.concatenate(
+        [
+            (gated_grad * x_part).astype(bf),
+            c_grad.astype(bf),
+            (gated_grad * b_part).astype(bf),
+        ],
+        axis=1,
+    )
+    in_weight_grad = dot(normed_full, projected_grad, 0, 0, bf).reshape(rows, depth, 3 * thin)
+    out_grad = dot(conv_out, attended_grad, 0, 0, bf)
+    few = jnp.concatenate(
+        [gain_two_local[None], kernel_local, jnp.zeros((4, width), jnp.float32)], axis=0
+    )
+    scattered = Scatter(dot(projected_grad, in_part, 1, 1, bf), team, cols)
+    normed_one_grad, totals, first_back, out_back = together(
+        6,
+        team,
+        cols,
+        scattered,
+        Totals(few, tok_float * inv_one, scattered, rows),
+        Wide(jnp.concatenate([in_weight_grad, grad_pieces[0]], axis=2), team, cols, False),
+        Tall(out_grad.reshape(depth, cols, width).transpose(1, 0, 2), team, cols, False),
+    )
+    token_back, _ = norm_backward(normed_one_grad, gain_one, tok_float, inv_one)
+    tokens_grad = middle_grad + token_back
+    wide_sum = jnp.concatenate(
+        [
+            jnp.sum(back.astype(jnp.float32).reshape(cols, team, depth, -1), axis=0)
+            for back in (first_back, second_back, third_back)
+        ],
+        axis=2,
+    )
+    in_grad = (
+        wide_sum[:, :, : 3 * thin]
+        .reshape(team, depth, 3, thin)
+        .transpose(1, 2, 0, 3)
+        .reshape(in_weight.shape)
+    )
+    gate_out = wide_sum[:, :, 3 * thin : 3 * thin + part].transpose(1, 0, 2).reshape(depth, inner)
+    up_out = wide_sum[:, :, 3 * thin + part :].transpose(1, 0, 2).reshape(depth, inner)
+    return (
+        block_out,
+        tokens_grad,
+        totals[7],
+        in_grad,
+        totals[1:4],
+        jnp.sum(out_back.astype(jnp.float32), axis=0),
+        totals[0],
+        gate_out,
+        up_out,
+        jnp.sum(down_back.astype(jnp.float32), axis=0),
+    )
+
+
 def solution(mesh):
     in_specs = (
         P("row", "col"),
@@ -193,4 +784,7 @@
         P("row", "col"),
         P("row", "col"),
     )
-    return jax.shard_map(local, mesh=mesh, in_specs=in_specs, out_specs=out_specs, check_vma=False)
+    rows, cols = mesh.shape["row"], mesh.shape["col"]
+    shared = cols > 1 and rows % cols == 0 and rows // cols > 1
+    body = teams if shared else local
+    return jax.shard_map(body, mesh=mesh, in_specs=in_specs, out_specs=out_specs, check_vma=False)

time: 1150 us -> 301 us (0.26)
  waiting for transfers between devices: 963 us -> 0.01 us
  Pallas kernels: 0 us -> 216 us
  blocking collectives: 95.5 us -> 10.2 us
  matrix products: 50.1 us -> 18.4 us
  local copies, waits for them, and re-layouts: 8.6 us -> 25.1 us
  between operations: 14.3 us -> 1.43 us
    reduce_scatter x8 -> x0, waiting for transfers between devices: 609 us -> none  [the longest x4 585 us: weight_terms(): lax.psum_scatter(jnp.einsum('tr,tkc->rkc', left, grad, preferred_element_...]
    all_gather x6 -> x0, waiting for transfers between devices: 345 us -> none  [the longest x1 83.4 us: local(): lax.all_gather(down_weight, 'row', axis=0, tiled=True)]
    pallas_call x0 -> x6, Pallas kernels: none -> 216 us  [together(): pl.pallas_call(functools.partial(together_kernel, team, cols, parts), out...]
    psum x1 -> x0, blocking collectives: 79.7 us -> none  [local(): lax.psum((gain_one_local, kernel_local, gain_two_local), 'row')]
    dot_general x12, matrix products: 50.1 us -> 18.4 us  [dot(): lax.dot_general(a, b, (((a_dim,), (b_dim,)), ((), ())), preferred_element...]
  transfers between devices with their start and end apart: 16 -> 2, of which waited for: 14 -> 0; matrix products, arithmetic and copies ran while one was open for 5% -> 3% of each run, Pallas kernels for 0% -> 0%
where the time goes in v2:
time: 301 us; the launch traced here: 298 us
  Pallas kernels  216 us (72%)
  local copies, waits for them, and re-layouts  25.1 us (8%)
  other arithmetic  21.1 us (7%)
  matrix products  18.4 us (6%)
  blocking collectives  10.2 us (3%)
  starting transfers between devices  6.56 us (2%)
    pallas_call x6, Pallas kernels, together(): pl.pallas_call(functools.partial(together_kernel, team, cols, parts), out...  216 us
    dot_general x12, matrix products, dot(): lax.dot_general(a, b, (((a_dim,), (b_dim,)), ((), ())), preferred_element...  18.4 us
    ppermute x2, starting transfers between devices, shifted(): return lax.ppermute(block, axis, route)  6.56 us
    unnamed x94, local copies, waits for them, and re-layouts  6.49 us
  transfers between devices with their start and end apart: 2, of which 0 were waited for; matrix products, arithmetic and copies ran while one was open for 3% of the time, Pallas kernels for 0%

profile of v2, /device:TPU:0, one launch (start us, length us, event | category | flops | bytes accessed | tf_op | source)
XLA Modules:
  0.0 298.4 jit_solution(9212723286548950322)
XLA Ops:
  0.7 1.1 fusion.13
  1.7 2.6 psum.28
  5.5 1.6 reshape.115
  7.1 1.6 reshape.118
  8.7 1.2 reshape.113
  11.2 31.2 %shard_map.186 = (bf16[1024,1024]{1,0:T(8,128)(2,1)S(1)}, bf16[16,64,256]{2,1,0:T(8,128)(2,1)S(1)}, bf16[2,64,512]{2,1,0:T(8,128)(2,1)S(1)}) custom-call(bf16[128,512]{1,0:T(8,128)(2,1)S(1)} %get-tuple-element.94.refs_0_, bf16[8,64,256]{2,1,0:T(8,128)(2,1)S(1)} %get-tuple-element.91.refs_1_, bf16[64,512]{1,0:T(8,128)(2,1)S(1)} %copy-done.11), custom_call_target="tpu_custom_call" | custom-call | tf_op jit(solution)/shard_map/pallas_call | solution.py:529
  43.9 5.3 %collective-permute-start = (f32[2,64]{0,1:T(8,128)S(1)}, f32[2,64]{0,1:T(8,128)S(1)}, u32[]{:S(2)}, u32[]{:S(2)}) collective-permute-start(f32[2,64]{0,1:T(8,128)S(1)} %slice.143), channel_id=1, source_target_pairs={{0,16},{2,18},{4,20},{6,22},{8,24},{10,26},{12,28},{14,30},{1,17},... | collective-permute-start | bytes 1544 | tf_op jit(solution)/shard_map/ppermute | solution.py:19
  54.6 34.7 %shard_map.187 = (f32[128,512]{1,0:T(8,128)S(1)}, bf16[1024,1024]{1,0:T(8,128)(2,1)S(1)}, bf16[16,64,256]{2,1,0:T(8,128)(2,1)S(1)}) custom-call(bf16[1024,1024]{1,0:T(8,128)(2,1)S(1)} %convolution_convert_fusion.2.refs_0_, bf16[128,512]{1,0:T(8,128)(2,1)S(1)} %copy-done.7, bf16[8,64,256]{2,1,0:T(8,128)(2,1)S(1)} %get-tuple-element.90.refs_2_), custom_call_target="tpu_custom_call" | custom-call | tf_op jit(solution)/shard_map/pallas_call | solution.py:529
  89.3 1.3 copy-done.12
  90.7 2.5 psum.29
  93.8 35.3 %shard_map.188 = (bf16[1024,1024]{1,0:T(8,128)(2,1)S(1)}, bf16[16,64,256]{2,1,0:T(8,128)(2,1)S(1)}, bf16[2,288,512]{2,1,0:T(8,128)(2,1)S(1)}) custom-call(bf16[128,512]{1,0:T(8,128)(2,1)S(1)} %multiply_convert_fusion.6.refs_0_, bf16[8,64,256]{2,1,0:T(8,128)(2,1)S(1)} %get-tuple-element.89.refs_1_, bf16[288,512]{1,0:T(8,128)(2,1)S(1)} %copy-done.10), custom_call_target="tpu_custom_call" | custom-call | tf_op jit(solution)/shard_map/pallas_call | solution.py:529
  129.2 3.1 %fusion.3 = f32[1024,576]{0,1:T(8,128)S(1)} fusion(bf16[1024,1024]{1,0:T(8,128)(2,1)S(1)} %get-tuple-element.33, bf16[1024,256]{1,0:T(8,128)(2,1)S(1)} %bitcast.96, bf16[1024,256]{1,0:T(8,128)(2,1)S(1)} %bitcast.94, bf16[1024,64]{1,0:T(8,128)(2,1)} %slice.147), kind=kOutput, calls=%fused_computation.24 | convolution fusion | flops 1211498496 | bytes 5636096 | tf_op jit(solution)/shard_map/dot_general | solution.py:542
  132.3 1.3 multiply_convert_fusion.1
  133.6 1.4 convolution_convert_fusion.4
  135.1 3.6 %convolution_convert_fusion.3.refs_0_ = bf16[1024,1024]{1,0:T(8,128)(2,1)} fusion(bf16[1024,288]{0,1:T(8,128)(2,1)S(1)} %get-tuple-element.83, bf16[1024,288]{0,1:T(8,128)(2,1)S(1)} %get-tuple-element.82, bf16[1024,256]{1,0:T(8,128)(2,1)S(1)} %bitcast.97, bf16[1024,256]{1,0:T(8,128)(2,1)S(1)} %bitcast.95, bf16[1024,64]{1,0:T(8,128)(2,1)S(1)} %copy-done.33), kind=kOutput, calls=%fused_computation.3 | convolution fusion | flops 1214906368 | bytes 4456448 | tf_op jit(solution)/shard_map/dot_general | solution.py:542
  139.5 2.6 convolution_convert_fusion.1.refs_0_
  143.2 1.6 copy-done.1
  144.8 30.6 %shard_map.189 = (f32[128,512]{1,0:T(8,128)S(1)}, bf16[16,64,256]{2,1,0:T(8,128)(2,1)S(1)}, bf16[2,288,512]{2,1,0:T(8,128)(2,1)S(1)}) custom-call(bf16[1024,1024]{1,0:T(8,128)(2,1)S(1)} %copy-done.1, bf16[16,64,256]{2,1,0:T(8,128)(2,1)S(1)} %bitcast.86, bf16[2,288,512]{2,1,0:T(8,128)(2,1)S(1)} %bitcast.85), custom_call_target="tpu_custom_call" | custom-call | tf_op jit(solution)/shard_map/pallas_call | solution.py:529
  177.6 2.7 psum.30
  180.8 1.2 copy.78
  182.1 1.9 fusion.30
  184.0 42.8 %shard_map.190 = (f32[128,512]{1,0:T(8,128)S(1)}, bf16[1024,1024]{1,0:T(8,128)(2,1)S(1)}, bf16[16,64,256]{2,1,0:T(8,128)(2,1)S(1)}) custom-call(bf16[1024,1024]{1,0:T(8,128)(2,1)S(1)} %copy-done, bf16[128,512]{1,0:T(8,128)(2,1)S(1)} %get-tuple-element.76.refs_1_, bf16[16,64,256]{2,1,0:T(8,128)(2,1)S(1)} %bitcast.87), custom_call_target="tpu_custom_call" | custom-call | tf_op jit(solution)/shard_map/pallas_call | solution.py:529
  226.9 1.1 convolution_convert_fusion.7
  228.9 2.0 multiply_reduce_fusion.1
  231.5 1.3 collective-permute-start.1
  238.9 1.5 multiply_convert_fusion.5
  241.4 1.3 convolution_convert_fusion.6
  243.5 2.0 copy.79
  245.5 1.2 pad_maximum_fusion.8.refs_3_
  246.8 41.0 %shard_map.191 = (f32[128,512]{1,0:T(8,128)S(1)}, f32[8,512]{1,0:T(8,128)S(1)}, bf16[16,64,256]{2,1,0:T(8,128)(2,1)S(1)}, bf16[2,64,512]{2,1,0:T(8,128)(2,1)S(1)}) custom-call(bf16[1024,1024]{1,0:T(8,128)(2,1)S(1)} %convolution_convert_fusion.refs_0_, f32[8,512]{1,0:T(8,128)S(1)} %maximum_maximum_fusion.refs_1_, f32[128,512]{1,0:T(8,128)S(1)} %get-tuple-element.93.refs_2_, ...), custom_call_target="tpu_custom_call" | custom-call | tf_op jit(solution)/shard_map/pallas_call | solution.py:529
  291.7 1.1 reshape.137
  294.4 2.5 psum.31
  (157 shorter events, 30.9 us)
Async XLA Ops:
  0.6 9.7 %copy-start.18 = (bf16[128,512]{1,0:T(8,128)(2,1)S(1)}, bf16[128,512]{1,0:T(8,128)(2,1)}, u32[]{:S(2)}) copy-start(bf16[128,512]{1,0:T(8,128)(2,1)} %param.11) | copy-start | bytes 393220
  4.8 5.8 %copy-start.43 = (f32[128]{0:T(128)}, f32[128]{0:T(128)S(1)}, u32[]{:S(2)}) copy-start(f32[128]{0:T(128)S(1)} %get-tuple-element.105) | copy-start | bytes 1540
  5.5 5.1 %copy-start.36 = (f32[512]{0:T(512)}, f32[512]{0:T(512)S(1)}, u32[]{:S(2)}) copy-start(f32[512]{0:T(512)S(1)} %convert_element_type.94) | copy-start | bytes 6148
  42.5 7.5 %copy-start.39 = (s32[2048]{0:T(1024)S(1)}, s32[2048]{0:T(1024)}, u32[]{:S(2)}) copy-start(s32[2048]{0:T(1024)} %param.12) | copy-start | bytes 24580
  42.5 9.1 %copy-start.45 = (bf16[512]{0:T(512)(128)(2,1)S(1)}, bf16[512]{0:T(512)(128)(2,1)}, u32[]{:S(2)}) copy-start(bf16[512]{0:T(512)(128)(2,1)} %param.17) | copy-start | bytes 3076
  43.4 9.8 %copy-start.14 = (f32[1024,192]{0,1:T(8,128)}, f32[1024,192]{0,1:T(8,128)S(1)}, u32[]{:S(2)}) copy-start(f32[1024,192]{0,1:T(8,128)S(1)} %fusion.5) | copy-start | bytes 2359300
  43.8 10.7 %copy-start.20 = (f32[1024,64]{0,1:T(8,128)}, f32[1024,64]{0,1:T(8,128)S(1)}, u32[]{:S(2)}) copy-start(f32[1024,64]{0,1:T(8,128)S(1)} %slice_multiply_fusion) | copy-start | bytes 786436
  43.9 8.3 %collective-permute-start = (f32[2,64]{0,1:T(8,128)S(1)}, f32[2,64]{0,1:T(8,128)S(1)}, u32[]{:S(2)}, u32[]{:S(2)}) collective-permute-start(f32[2,64]{0,1:T(8,128)S(1)} %slice.143), channel_id=1, source_target_pairs={{0,16},{2,18},{4,20},{6,22},{8,24},{10,26},{12,28},{14,30},{1,17},... | collective-permute-start | bytes 1544 | tf_op jit(solution)/shard_map/ppermute | solution.py:19
  49.9 4.6 %copy-start.40 = (f32[64]{0:T(128)}, f32[64]{0:T(128)S(1)}, u32[]{:S(2)}) copy-start(f32[64]{0:T(128)S(1)} %get-tuple-element.101) | copy-start | bytes 772
  50.0 4.6 %copy-start.41 = (f32[64]{0:T(128)}, f32[64]{0:T(128)S(1)}, u32[]{:S(2)}) copy-start(f32[64]{0:T(128)S(1)} %get-tuple-element.102) | copy-start | bytes 772
  50.0 4.6 %copy-start.42 = (f32[64]{0:T(128)}, f32[64]{0:T(128)S(1)}, u32[]{:S(2)}) copy-start(f32[64]{0:T(128)S(1)} %get-tuple-element.103) | copy-start | bytes 772
  50.0 4.6 %copy-start.7 = (bf16[128,512]{1,0:T(8,128)(2,1)S(1)}, bf16[128,512]{1,0:T(8,128)(2,1)}, u32[]{:S(2)}) copy-start(bf16[128,512]{1,0:T(8,128)(2,1)} %refs_1_.1) | copy-start | bytes 393220
  51.6 37.7 %copy-start.25 = (bf16[2,8,8,512]{3,2,0,1:T(8,128)(2,1)}, bf16[2,8,8,512]{3,2,0,1:T(8,128)(2,1)S(1)}, u32[]{:S(2)}) copy-start(bf16[2,8,8,512]{3,2,0,1:T(8,128)(2,1)S(1)} %copy.88) | copy-start | bytes 393220
  52.2 37.1 %copy-start.34 = (f32[2,64]{0,1:T(8,128)}, f32[2,64]{0,1:T(8,128)S(1)}, u32[]{:S(2)}) copy-start(f32[2,64]{0,1:T(8,128)S(1)} %collective-permute-done) | copy-start | bytes 1540
  54.6 39.3 %copy-start.10 = (bf16[288,512]{1,0:T(8,128)(2,1)S(1)}, bf16[288,512]{1,0:T(8,128)(2,1)}, u32[]{:S(2)}) copy-start(bf16[288,512]{1,0:T(8,128)(2,1)} %refs_2_.3) | copy-start | bytes 884740
  90.7 38.5 %copy-start.15 = (f32[128,512]{1,0:T(8,128)}, f32[128,512]{1,0:T(8,128)S(1)}, u32[]{:S(2)}) copy-start(f32[128,512]{1,0:T(8,128)S(1)} %get-tuple-element.79) | copy-start | bytes 786436
  135.1 7.1 %copy-start.29 = (bf16[1024,576]{0,1:T(8,128)(2,1)}, bf16[1024,576]{0,1:T(8,128)(2,1)S(1)}, u32[]{:S(2)}) copy-start(bf16[1024,576]{0,1:T(8,128)(2,1)S(1)} %convolution_convert_fusion.4) | copy-start | bytes 3538948
  143.0 34.0 %copy-start.16 = (f32[128,512]{1,0:T(8,128)S(1)}, f32[128,512]{1,0:T(8,128)}, u32[]{:S(2)}) copy-start(f32[128,512]{1,0:T(8,128)} %copy-done.15) | copy-start | bytes 786436
  176.2 7.8 %copy-start = (bf16[1024,1024]{1,0:T(8,128)(2,1)S(1)}, bf16[1024,1024]{1,0:T(8,128)(2,1)}, u32[]{:S(2)}) copy-start(bf16[1024,1024]{1,0:T(8,128)(2,1)} %convolution_convert_fusion.1.refs_0_) | copy-start | bytes 6291460
  182.1 44.8 %copy-start.28 = (bf16[1024,64]{0,1:T(8,128)(2,1)S(1)}, bf16[1024,64]{0,1:T(8,128)(2,1)}, u32[]{:S(2)}) copy-start(bf16[1024,64]{0,1:T(8,128)(2,1)} %copy-done.27) | copy-start | bytes 393220
  184.0 44.0 %copy-start.26 = (bf16[2,8,8,512]{3,2,0,1:T(8,128)(2,1)S(1)}, bf16[2,8,8,512]{3,2,0,1:T(8,128)(2,1)}, u32[]{:S(2)}) copy-start(bf16[2,8,8,512]{3,2,0,1:T(8,128)(2,1)} %copy-done.25) | copy-start | bytes 393220
  228.1 5.6 %copy-start.17 = (f32[128,512]{1,0:T(8,128)S(1)}, f32[128,512]{1,0:T(8,128)}, u32[]{:S(2)}) copy-start(f32[128,512]{1,0:T(8,128)} %copy-done.15) | copy-start | bytes 786436
  228.8 5.6 %copy-start.6 = (bf16[2,288,512]{2,1,0:T(8,128)(2,1)S(1)}, bf16[2,288,512]{2,1,0:T(8,128)(2,1)}, u32[]{:S(2)}) copy-start(bf16[2,288,512]{2,1,0:T(8,128)(2,1)} %copy-done.5) | copy-start | bytes 1769476
  228.9 8.0 %copy-start.9 = (bf16[16,64,256]{2,1,0:T(8,128)(2,1)S(1)}, bf16[16,64,256]{2,1,0:T(8,128)(2,1)}, u32[]{:S(2)}) copy-start(bf16[16,64,256]{2,1,0:T(8,128)(2,1)} %copy-done.8) | copy-start | bytes 1572868
  231.5 7.4 %collective-permute-start.1 = (f32[2,64]{0,1:T(8,128)}, f32[2,64]{0,1:T(8,128)}, u32[]{:S(2)}, u32[]{:S(2)}) collective-permute-start(f32[2,64]{0,1:T(8,128)} %slice.152), channel_id=1, source_target_pairs={{16,0},{18,2},{20,4},{22,6},{24,8},{26,10},{28,12},{30,14},{17,1},... | collective-permute-start | bytes 1544 | tf_op jit(solution)/shard_map/ppermute | solution.py:19
  232.8 5.9 %slice-start = ((bf16[1024,576]{0,1:T(8,128)(2,1)}), bf16[1024,64]{0,1:T(8,128)(2,1)S(1)}, s32[]{:S(2)}) async-start(bf16[1024,576]{0,1:T(8,128)(2,1)} %copy-done.29), calls=%async_computation | async-start | bytes 262144 | tf_op jit(solution)/shard_map/slice | solution.py:664
  235.3 6.1 %copy-start.3 = (bf16[1024,1024]{1,0:T(8,128)(2,1)S(1)}, bf16[1024,1024]{1,0:T(8,128)(2,1)}, u32[]{:S(2)}) copy-start(bf16[1024,1024]{1,0:T(8,128)(2,1)} %copy-done.2) | copy-start | bytes 6291460
  246.7 42.3 %copy-start.22 = (f32[8,64,256]{2,1,0:T(8,128)S(1)}, f32[8,64,256]{2,1,0:T(8,128)}, u32[]{:S(2)}) copy-start(f32[8,64,256]{2,1,0:T(8,128)} %convert_reduce_fusion.2) | copy-start | bytes 1572868
  246.8 42.3 %copy-start.23 = (f32[8,64,256]{2,1,0:T(8,128)S(1)}, f32[8,64,256]{2,1,0:T(8,128)}, u32[]{:S(2)}) copy-start(f32[8,64,256]{2,1,0:T(8,128)} %convert_reduce_fusion.1) | copy-start | bytes 1572868
  292.8 4.8 %copy-start.30 = (f32[128,512]{1,0:T(8,128)S(1)}, f32[128,512]{1,0:T(8,128)}, u32[]{:S(2)}) copy-start(f32[128,512]{1,0:T(8,128)} %get-tuple-element.77) | copy-start | bytes 786436
  292.8 4.8 %copy-start.44 = (f32[128]{0:T(128)S(1)}, f32[128]{0:T(128)}, u32[]{:S(2)}) copy-start(f32[128]{0:T(128)} %copy-done.43) | copy-start | bytes 1540
  292.8 4.8 %copy-start.46 = (f32[128]{0:T(128)S(1)}, f32[128]{0:T(128)}, u32[]{:S(2)}) copy-start(f32[128]{0:T(128)} %get-tuple-element.104) | copy-start | bytes 1540
  (18 other events, 29.9 us)
